TPU v7x, 512 devices: a whole 4x8x8 slice. The times are simulated.
512 devices in a mesh: band: 32 (over y, x), grp: 16 (over z, core).
Axes of the slice: x: 4, y: 8, z: 8, core: 2. Of those that a mesh axis runs over, the one named last changes fastest.
Arguments:
- tokens: bfloat16 [4096, 48, 384], P(('band', 'grp')), may hold values from -6 to 6
- cotangent: bfloat16 [4096, 48, 384], P(('band', 'grp')), may hold values from -6 to 6
- ocean_mask: int32 [4096, 48], P(('band', 'grp')), may hold values 0 or 1
- land_mask: int32 [512, 6], P(('band', 'grp')), may hold values from 0 to 1, as said below
- w_qkv: bfloat16 [384, 1152], replicated, may hold values from -0.3125 to 0.3125
- w_proj: bfloat16 [384, 384], replicated, may hold values from -0.3125 to 0.3125
- rel_bias: float32 [12, 64, 64], replicated, may hold values from -4 to 345
Outputs:
- block_out: bfloat16 [4096, 48, 384], P(('band', 'grp'))
- token_grad: bfloat16 [4096, 48, 384], P(('band', 'grp'))
- grad_qkv: float32 [442368], P(('band', 'grp'))
- grad_proj: float32 [147456], P(('band', 'grp'))
- grad_bias: float32 [49152], P(('band', 'grp'))
Inputs may be any that keep to these rules, and one draw needn't show every extreme that they name: `land_mask`: for every r < 256 the windows with land flag 0 in rows r and r + 256 together number at most 8, exactly 8 for r = 0.
All inputs are finite; a program needn't handle non-finite values. No bound on the sum of `ocean_mask` on one device may be relied on, other than what follows from the above.
Results may differ from a plain program's by a relative error of at most 0.0091.
Values may be sent and summed in bfloat16 or wider, within the bound.
A program may use at most 64 MiB of HBM per device.

v0:
```python
import math

import jax
import jax.numpy as jnp
from jax import lax
from jax.sharding import PartitionSpec as P

epsilon = 1e-05
masked_score = -1e30


def from_behind(block, axis, distance):
    devices = range(lax.axis_size(axis))
    route = [(i - distance, i) for i in devices if i - distance in devices]
    return lax.ppermute(block, axis, route)


def window_pass(window_in, window_cot, window_mask, w_qkv, w_proj, rel_bias):
    channels = window_in.shape[-1]
    head_count = rel_bias.shape[0]
    head_size = channels // head_count
    number = window_in.shape[0]
    score_scale = 1.0 / math.sqrt(head_size)
    values_in = window_in.astype(jnp.float32)
    average = jnp.mean(values_in, -1, keepdims=True)
    centered = values_in - average
    inv_std = lax.rsqrt(jnp.mean(centered * centered, -1, keepdims=True) + epsilon)
    normed = centered * inv_std
    hidden = normed.astype(jnp.bfloat16).reshape(-1, channels)
    qkv = jnp.dot(hidden, w_qkv, preferred_element_type=jnp.float32).astype(jnp.bfloat16)
    qkv = qkv.reshape(number, 64, 3, head_count, head_size)
    queries = qkv[:, :, 0]
    key_rows = qkv[:, :, 1]
    values = qkv[:, :, 2]
    scores = jnp.einsum("bqhd,bkhd->bhqk", queries, key_rows, preferred_element_type=jnp.float32)
    scores = scores * score_scale + rel_bias[None]
    key_live = window_mask[:, None, None, :] > 0.5
    scores = jnp.where(key_live, scores, masked_score)
    row_max = jnp.max(scores, -1, keepdims=True)
    weights = jnp.exp(scores - row_max)
    probs = weights / jnp.sum(weights, -1, keepdims=True)
    probs_low = probs.astype(jnp.bfloat16)
    attended = jnp.einsum("bhqk,bkhd->bqhd", probs_low, values, preferred_element_type=jnp.float32)
    attended = attended.astype(jnp.bfloat16).reshape(-1, channels)
    projected = jnp.dot(attended, w_proj, preferred_element_type=jnp.float32)
    query_mask = window_mask.reshape(-1, 1)
    update = (query_mask * projected).astype(jnp.bfloat16)
    out_grad = (query_mask * window_cot.reshape(-1, channels).astype(jnp.float32)).astype(
        jnp.bfloat16
    )
    grad_proj = jnp.dot(attended.T, out_grad, preferred_element_type=jnp.float32)
    attended_grad = jnp.dot(out_grad, w_proj.T, preferred_element_type=jnp.float32).astype(
        jnp.bfloat16
    )
    attended_grad = attended_grad.reshape(number, 64, head_count, head_size)
    probs_grad = jnp.einsum(
        "bqhd,bkhd->bhqk", attended_grad, values, preferred_element_type=jnp.float32
    )
    values_grad = jnp.einsum(
        "bhqk,bqhd->bkhd", probs_low, attended_grad, preferred_element_type=jnp.float32
    ).astype(jnp.bfloat16)
    scores_grad = probs * (probs_grad - jnp.sum(probs * probs_grad, -1, keepdims=True))
    grad_bias = jnp.sum(scores_grad, 0)
    scaled_grad = (scores_grad * score_scale).astype(jnp.bfloat16)
    queries_grad = jnp.einsum(
        "bhqk,bkhd->bqhd", scaled_grad, key_rows, preferred_element_type=jnp.float32
    ).astype(jnp.bfloat16)
    keys_grad = jnp.einsum(
        "bhqk,bqhd->bkhd", scaled_grad, queries, preferred_element_type=jnp.float32
    ).astype(jnp.bfloat16)
    qkv_grad = jnp.stack([queries_grad, keys_grad, values_grad], axis=2).reshape(-1, 3 * channels)
    grad_qkv = jnp.dot(hidden.T, qkv_grad, preferred_element_type=jnp.float32)
    hidden_grad = jnp.dot(qkv_grad, w_qkv.T, preferred_element_type=jnp.float32).reshape(
        number, 64, channels
    )
    window_grad = inv_std * (
        hidden_grad
        - jnp.mean(hidden_grad, -1, keepdims=True)
        - normed * jnp.mean(hidden_grad * normed, -1, keepdims=True)
    )
    return (
        update.reshape(number, 64, channels),
        window_grad.astype(jnp.bfloat16),
        grad_qkv,
        grad_proj,
        grad_bias,
    )


def local_windows(grid):
    rolled = jnp.roll(grid, -4, axis=1)
    band_cols = rolled.shape[1] // 8
    tail = rolled.shape[2:]
    blocks = rolled.reshape((8, band_cols, 8) + tail)
    blocks = jnp.moveaxis(blocks, 1, 0)
    return blocks.reshape((band_cols, 64) + tail)


def local_grid(blocks):
    band_cols = blocks.shape[0]
    tail = blocks.shape[2:]
    grid = blocks.reshape((band_cols, 8, 8) + tail)
    grid = jnp.moveaxis(grid, 1, 0).reshape((8, band_cols * 8) + tail)
    return jnp.roll(grid, 4, axis=1)


def local(tokens, cotangent, ocean_mask, land_mask, w_qkv, w_proj, rel_bias):
    ocean_low = ocean_mask.astype(jnp.bfloat16)
    upper_x, upper_g, upper_m = from_behind(
        (tokens[:4], cotangent[:4], ocean_low[:4]), ("band", "grp"), -1
    )
    windows_x = local_windows(jnp.concatenate([tokens[4:], upper_x], 0))
    windows_g = local_windows(jnp.concatenate([cotangent[4:], upper_g], 0))
    windows_m = local_windows(jnp.concatenate([ocean_low[4:], upper_m], 0)).astype(jnp.float32)
    windows_m = windows_m * (1.0 - land_mask[0].astype(jnp.float32))[:, None]
    update, window_grad, part_qkv, part_proj, part_bias = window_pass(
        windows_x, windows_g, windows_m, w_qkv, w_proj, rel_bias
    )
    grid_update = local_grid(update)
    grid_grad = local_grid(window_grad)
    lower_update, lower_grad = from_behind((grid_update[4:], grid_grad[4:]), ("band", "grp"), 1)
    full_update = jnp.concatenate([lower_update, grid_update[:4]], 0)
    full_grad = jnp.concatenate([lower_grad, grid_grad[:4]], 0)
    block_out = (tokens.astype(jnp.float32) + full_update.astype(jnp.float32)).astype(jnp.bfloat16)
    token_grad = (cotangent.astype(jnp.float32) + full_grad.astype(jnp.float32)).astype(
        jnp.bfloat16
    )
    partials = (part_qkv.reshape(-1), part_proj.reshape(-1), part_bias.reshape(-1))
    sum_qkv, sum_proj, sum_bias = (
        lax.psum_scatter(partials[0], ("band", "grp"), scatter_dimension=0, tiled=True),
        lax.psum_scatter(partials[1], ("band", "grp"), scatter_dimension=0, tiled=True),
        lax.psum_scatter(partials[2], ("band", "grp"), scatter_dimension=0, tiled=True),
    )
    return (block_out, token_grad, sum_qkv, sum_proj, sum_bias)


def solution(mesh):
    placed = (
        P(("band", "grp"), None, None),
        P(("band", "grp"), None, None),
        P(("band", "grp"), None),
        P(("band", "grp"), None),
        P(),
        P(),
        P(),
    )
    return jax.shard_map(
        local,
        mesh=mesh,
        in_specs=placed,
        out_specs=(
            P(("band", "grp"), None, None),
            P(("band", "grp"), None, None),
            P(("band", "grp")),
            P(("band", "grp")),
            P(("band", "grp")),
        ),
        check_vma=False,
    )
```

profile of v0, /device:TPU:1, one launch (start us, length us, event | category | flops | bytes accessed | tf_op | source)
XLA Modules:
  0.0 378.5 jit_solution(949652810759794614)
XLA Ops:
  8.0 8.8 %collective-permute-start = (bf16[4,48]{1,0:T(4,128)(2,1)S(1)}, bf16[4,48]{1,0:T(4,128)(2,1)S(1)}, u32[]{:S(2)}, u32[]{:S(2)}) collective-permute-start(bf16[4,48]{1,0:T(4,128)(2,1)S(1)} %get-tuple-element.18), channel_id=1, source_target_pairs={{1,0},{2,1},{3,2},{4,3},{5,4},{6,5},{7,6},{8,7},{9,8},{10,9},{11,1... | collective-permute-start | bytes 1160 | tf_op jit(solution)/shard_map/ppermute | solution.py:15
  17.8 1.9 collective-permute-start.1
  20.8 1.9 collective-permute-start.3
  23.5 1.9 copy.103
  32.8 3.0 reshape.191
  35.7 1.6 fusion.44
  37.3 4.2 %fusion.48 = (f32[6,12,64]{2,1,0:T(8,128)S(1)}, f32[6,12,64,64]{2,3,1,0:T(8,128)}) fusion(f32[12,64,64]{1,2,0:T(8,128)} %copy.103, pred[6,64]{1,0:T(8,128)(4,1)S(1)} %multiply_compare_fusion, bf16[6,64,1,12,32]{1,0,4,3,2:T(8,128)(2,1)} %get-tuple-element.10, bf16[6,64,1,12,32]{1,0,4,3,2:T(8,128)(2,1)} %get-tuple-element.11), kind=kOutput, calls=%fused_computation.96 | convolution fusion | flops 20348992 | bytes 1984896 | tf_op jit(solution)/shard_map/sub | solution.py:40
  41.5 2.5 fusion.9
  45.1 3.7 fusion.49
  50.9 1.5 copy.114
  54.9 2.3 reshape.192
  57.3 2.1 fusion.10
  60.6 2.1 fusion.51
  62.7 1.9 reshape.199
  67.0 3.8 %collective-permute-start.2 = (bf16[4,48,384]{2,1,0:T(8,128)(2,1)}, bf16[4,48,384]{2,1,0:T(8,128)(2,1)}, u32[]{:S(2)}, u32[]{:S(2)}) collective-permute-start(bf16[4,48,384]{2,1,0:T(8,128)(2,1)} %fusion.38), channel_id=1, source_target_pairs={{0,1},{1,2},{2,3},{3,4},{4,5},{5,6},{6,7},{7,8},{8,9},{9,10},{10,1... | collective-permute-start | bytes 442376 | tf_op jit(solution)/shard_map/ppermute | solution.py:15
  70.9 1.9 copy.119
  72.8 1.8 reshape.200
  74.6 2.4 reshape.197
  78.0 3.1 fusion.50
  81.1 2.7 reshape.198
  85.5 2.4 collective-permute-start.4
  87.9 1.7 add_convert_fusion.1
  90.8 276.9 %all-reduce.6.cloned.1.call-done = (f32[442368]{0:T(1024)}, f32[147456]{0:T(1024)}, f32[49152]{0:T(1024)}) async-done(((f32[442368]{0:T(1024)}, f32[147456]{0:T(1024)}, f32[49152]{0:T(1024)}), (f32[442368]{0:T(1024)}, f32[147456]{0:T(1024)}, f32[49152]{0:T(1024)})) %all-reduce.6.cloned.1.call-update) | async-done | bytes 2555920
  368.9 1.4 dynamic-slice
  (112 shorter events, 26.2 us)
Async XLA Ops:
  7.2 23.6 %copy-start = (bf16[384,1152]{1,0:T(8,128)(2,1)S(1)}, bf16[384,1152]{1,0:T(8,128)(2,1)}, u32[]{:S(2)}) copy-start(bf16[384,1152]{1,0:T(8,128)(2,1)} %param.11) | copy-start | bytes 2654212
  7.2 360.5 %all-reduce.6.cloned.1.call-start = ((), (), s32[]{:S(2)}) async-start(), calls=%async_computation | async-start | bytes 5111808
  8.0 17.4 %collective-permute-start = (bf16[4,48]{1,0:T(4,128)(2,1)S(1)}, bf16[4,48]{1,0:T(4,128)(2,1)S(1)}, u32[]{:S(2)}, u32[]{:S(2)}) collective-permute-start(bf16[4,48]{1,0:T(4,128)(2,1)S(1)} %get-tuple-element.18), channel_id=1, source_target_pairs={{1,0},{2,1},{3,2},{4,3},{5,4},{6,5},{7,6},{8,7},{9,8},{10,9},{11,1... | collective-permute-start | bytes 1160 | tf_op jit(solution)/shard_map/ppermute | solution.py:15
  17.8 12.7 %copy-start.1 = (bf16[4,48,384]{2,1,0:T(8,128)(2,1)}, bf16[4,48,384]{2,1,0:T(8,128)(2,1)S(1)}, u32[]{:S(2)}) copy-start(bf16[4,48,384]{2,1,0:T(8,128)(2,1)S(1)} %get-tuple-element.15) | copy-start | bytes 442372
  17.8 8.8 %collective-permute-start.1 = (bf16[4,48,384]{2,1,0:T(8,128)(2,1)S(1)}, bf16[4,48,384]{2,1,0:T(8,128)(2,1)S(1)}, u32[]{:S(2)}, u32[]{:S(2)}) collective-permute-start(bf16[4,48,384]{2,1,0:T(8,128)(2,1)S(1)} %get-tuple-element.16), channel_id=1, source_target_pairs={{1,0},{2,1},{3,2},{4,3},{5,4},{6,5},{7,6},{8,7},{9,8},{10,9},{11,1... | collective-permute-start | bytes 442376 | tf_op jit(solution)/shard_map/ppermute | solution.py:15
  20.8 7.6 %copy-start.13 = (bf16[4,48,384]{2,1,0:T(8,128)(2,1)}, bf16[4,48,384]{2,1,0:T(8,128)(2,1)S(1)}, u32[]{:S(2)}) copy-start(bf16[4,48,384]{2,1,0:T(8,128)(2,1)S(1)} %get-tuple-element.13) | copy-start | bytes 442372
  20.8 6.8 %collective-permute-start.3 = (bf16[4,48,384]{2,1,0:T(8,128)(2,1)S(1)}, bf16[4,48,384]{2,1,0:T(8,128)(2,1)S(1)}, u32[]{:S(2)}, u32[]{:S(2)}) collective-permute-start(bf16[4,48,384]{2,1,0:T(8,128)(2,1)S(1)} %get-tuple-element.14), channel_id=1, source_target_pairs={{1,0},{2,1},{3,2},{4,3},{5,4},{6,5},{7,6},{8,7},{9,8},{10,9},{11,1... | collective-permute-start | bytes 442376 | tf_op jit(solution)/shard_map/ppermute | solution.py:15
  26.6 3.9 %copy-start.3 = (bf16[4,48,384]{2,1,0:T(8,128)(2,1)}, bf16[4,48,384]{2,1,0:T(8,128)(2,1)S(1)}, u32[]{:S(2)}) copy-start(bf16[4,48,384]{2,1,0:T(8,128)(2,1)S(1)} %collective-permute-done.1) | copy-start | bytes 442372
  26.9 1.7 copy-start.19
  26.9 1.6 copy-start.17
  27.5 1.4 copy-start.14
  37.3 4.2 %copy-start.12 = (bf16[6,64,12,32]{1,0,3,2:T(8,128)(2,1)S(1)}, bf16[6,64,12,32]{1,0,3,2:T(8,128)(2,1)}, u32[]{:S(2)}) copy-start(bf16[6,64,12,32]{1,0,3,2:T(8,128)(2,1)} %reshape.194) | copy-start | bytes 884740
  41.5 2.5 copy-start.11
  41.5 2.6 copy-start.22
  45.1 3.7 copy-start.10
  67.0 20.9 %collective-permute-start.2 = (bf16[4,48,384]{2,1,0:T(8,128)(2,1)}, bf16[4,48,384]{2,1,0:T(8,128)(2,1)}, u32[]{:S(2)}, u32[]{:S(2)}) collective-permute-start(bf16[4,48,384]{2,1,0:T(8,128)(2,1)} %fusion.38), channel_id=1, source_target_pairs={{0,1},{1,2},{2,3},{3,4},{4,5},{5,6},{6,7},{7,8},{8,9},{9,10},{10,1... | collective-permute-start | bytes 442376 | tf_op jit(solution)/shard_map/ppermute | solution.py:15
  81.1 2.7 copy-start.2
  81.1 2.7 copy-start.4
  81.1 2.7 copy-start.5
  83.8 4.1 %copy-start.7 = (bf16[8,6,8,384]{3,2,1,0:T(8,128)(2,1)S(1)}, bf16[8,6,8,384]{3,2,1,0:T(8,128)(2,1)}, u32[]{:S(2)}) copy-start(bf16[8,6,8,384]{3,2,1,0:T(8,128)(2,1)} %copy-done.6) | copy-start | bytes 884740
  83.8 4.1 %copy-start.15 = (bf16[8,48,384]{2,1,0:T(8,128)(2,1)S(1)}, bf16[8,48,384]{2,1,0:T(8,128)(2,1)}, u32[]{:S(2)}) copy-start(bf16[8,48,384]{2,1,0:T(8,128)(2,1)} %param.7) | copy-start | bytes 884740
  83.8 4.1 %copy-start.21 = (bf16[8,4,384]{2,1,0:T(4,128)(2,1)S(1)}, bf16[8,4,384]{2,1,0:T(4,128)(2,1)}, u32[]{:S(2)}) copy-start(bf16[8,4,384]{2,1,0:T(4,128)(2,1)} %copy-done.20) | copy-start | bytes 73732
  85.1 4.9 %copy-start.16 = (bf16[8,48,384]{2,1,0:T(8,128)(2,1)S(1)}, bf16[8,48,384]{2,1,0:T(8,128)(2,1)}, u32[]{:S(2)}) copy-start(bf16[8,48,384]{2,1,0:T(8,128)(2,1)} %param.8) | copy-start | bytes 884740
  85.5 4.5 %collective-permute-start.4 = (bf16[4,48,384]{2,1,0:T(8,128)(2,1)S(1)}, bf16[4,48,384]{2,1,0:T(8,128)(2,1)S(1)}, u32[]{:S(2)}, u32[]{:S(2)}) collective-permute-start(bf16[4,48,384]{2,1,0:T(8,128)(2,1)S(1)} %fusion.37), channel_id=1, source_target_pairs={{0,1},{1,2},{2,3},{3,4},{4,5},{5,6},{6,7},{7,8},{8,9},{9,10},{10,1... | collective-permute-start | bytes 442376 | tf_op jit(solution)/shard_map/ppermute | solution.py:15
  (5 other events, 5.1 us)
Sparse Core Ops, SparseCore 0:
  83.9 283.7 all-reduce.5
where the time goes:
time: 380 us; the launch traced here: 378 us
  waiting for transfers between devices  277 us (73%)
  local copies, waits for them, and re-layouts  37 us (10%)
  starting transfers between devices  18.9 us (5%)
  matrix products  18.4 us (5%)
  between operations  14.5 us (4%)
  other arithmetic  12.5 us (3%)
    unnamed x2, waiting for transfers between devices  277 us
    ppermute x5, starting transfers between devices, from_behind(): return lax.ppermute(block, axis, route)  18.8 us
    unnamed x50, local copies, waits for them, and re-layouts  7.85 us
  transfers between devices with their start and end apart: 6, of which 2 were waited for; matrix products, arithmetic and copies ran while one was open for 6% of the time, Pallas kernels for 0%

commit v1 on v0

v1 whole, which is shorter than its diff:
```python
import math

import jax
import jax.numpy as jnp
from jax import lax
from jax.experimental import pallas as pl
from jax.experimental.pallas import tpu as pltpu
from jax.sharding import PartitionSpec as P

EPS = 1e-05
MASKED = -1e30
C = 384
WB = 6
HG = 3
SCALE = 1.0 / math.sqrt(32)
F32 = jnp.float32
BF16 = jnp.bfloat16
MESH = pl.DeviceIdType.MESH

NY, NX, NZ = 8, 4, 8
OWN = 192


def qkv_rows(g):
    return [("qkv", j, k) for j in range(3) for k in (g, 3 + g, 6 + g)]


PROJ_ROWS = [("proj", j, k) for j in range(3) for k in range(3)]
BIAS_ROWS = [("bias", j, 0) for j in range(3)]
PARTS = [
    (qkv_rows(0) + PROJ_ROWS[:7], 16, 16),
    (qkv_rows(1) + qkv_rows(2) + PROJ_ROWS[7:] + BIAS_ROWS, 24, 16),
]


def place_of(kind, j, k):
    return {"qkv": 9 * j + k, "proj": 27 + 3 * j + k, "bias": 36 + j}[kind]


def dot_nt(a, b):
    return lax.dot_general(a, b, (((1,), (1,)), ((), ())), preferred_element_type=F32)


def dot_tn(a, b):
    return lax.dot_general(a, b, (((0,), (0,)), ((), ())), preferred_element_type=F32)


def dot_nn(a, b):
    return lax.dot_general(a, b, (((1,), (0,)), ((), ())), preferred_element_type=F32)


def stage_mask(ocean, land, half, mask_ref):
    place = lax.broadcasted_iota(jnp.int32, (8, 48), 0)
    column = lax.broadcasted_iota(jnp.int32, (8, 48), 1)
    for w in range(WB):
        live = 1.0 - land[:, w : w + 1]
        pick = (column == lax.rem(place + (8 * w + 4), 48)).astype(F32) * live
        for i in range(4):
            row = jnp.broadcast_to(ocean[i : i + 1, :], (8, 48))
            value = jnp.sum(row * pick, axis=1, keepdims=True)
            at = OWN * half + 32 * w + 8 * i
            mask_ref[at : at + 8, :] = jnp.broadcast_to(value, (8, 128))


def stage_rows(rows, half, out_ref):
    for i, row in enumerate(rows):
        rolled = pltpu.roll(row.astype(F32), 44, 0)
        for w in range(WB):
            at = OWN * half + 32 * w + 8 * i
            out_ref[at : at + 8, :] = rolled[8 * w : 8 * w + 8, :]


def grid_row(src_ref, half, i):
    ats = [OWN * half + 32 * w + 8 * i for w in range(WB)]
    return pltpu.roll(jnp.concatenate([src_ref[at : at + 8, :] for at in ats], 0), 4, 0)


class Part:
    def __init__(self, rows, count, along_y, refs, here, send, sources, red_ref):
        (
            self.pk, self.pack, self.r0, self.s1, self.ra, self.ta, self.ra2, self.rb, self.tb, self.rb2,
            self.f, self.r3, self.tot, self.core_s, self.core_r, self.a1_s, self.a1_r, self.a2_s, self.a2_r,
            self.b1_s, self.b1_r, self.b2_s, self.b2_r, self.z_s, self.z_r,
        ) = refs
        self.rows, self.count, self.na = rows, count, along_y
        self.half = 2 * count
        self.nb = self.half - along_y
        self.here, self.send, self.sources, self.red = here, send, sources, red_ref
        self.sent = []

    def start(self):
        band, grp, y, x, z, core = self.here
        n = self.count
        grad_ref, bt_ref = self.sources
        lane = lax.broadcasted_iota(jnp.int32, (128, 128), 1)
        for i, (kind, j, k) in enumerate(self.rows):
            if kind == "bias":
                even = bt_ref[pl.ds(2 * j, 128, stride=6), :]
                odd = bt_ref[pl.ds(2 * j + 1, 128, stride=6), :]
                value = jnp.where(lane < 64, even, pltpu.roll(odd, 64, 1))
            else:
                at = k if kind == "qkv" else 9 + k
                value = grad_ref.at[at][pl.ds(j, 128, stride=3), :]
            self.pk[pl.ds(i, 128, stride=n), :] = value
        for i in range(len(self.rows), n):
            self.pk[pl.ds(i, 128, stride=n), :] = jnp.zeros((128, 128), F32)
        theirs = (1 - core) * self.half

        def narrow(i, carry):
            for j in range(NX):
                at = pl.multiple_of((i * NX + j) * 4 * n + theirs, 16)
                self.pack[i, j] = self.pk[pl.ds(at, self.half), :].astype(BF16)
            return carry

        lax.fori_loop(0, NY, narrow, 0)
        self.core_copy = self.send(
            self.pack, self.r0, self.core_s.at[0], self.core_r.at[0], (band, z * 2 + 1 - core)
        )

    def spread(self):
        band, grp, y, x, z, core = self.here
        n, na = self.count, self.na
        mine = core * self.half
        self.core_copy.wait()

        def add(i, carry):
            for j in range(NX):
                at = pl.multiple_of((i * NX + j) * 4 * n + mine, 16)
                total = self.pk[pl.ds(at, self.half), :] + self.r0[i, j].astype(F32)
                self.s1[i, j] = total.astype(BF16)
            return carry

        lax.fori_loop(0, NY, add, 0)
        self.b1, self.a1 = [], []
        for d in range(1, NX):
            to = lax.rem(x + d, NX)
            self.b1.append(
                self.send(
                    self.s1.at[:, to, pl.ds(na, self.nb), :], self.rb.at[d - 1],
                    self.b1_s.at[d - 1], self.b1_r.at[d - 1], (y * NX + to, grp),
                )
            )
        for d in range(1, NY):
            to = lax.rem(y + d, NY)
            self.a1.append(
                self.send(
                    self.s1.at[to, :, pl.ds(0, na), :], self.ra.at[d - 1],
                    self.a1_s.at[d - 1], self.a1_r.at[d - 1], (to * NX + x, grp),
                )
            )

    def turn(self):
        band, grp, y, x, z, core = self.here
        na = self.na
        total = self.s1[:, x, na : self.half, :].astype(F32)
        for d in range(1, NX):
            self.b1[d - 1].wait_recv()
            total = total + self.rb[d - 1].astype(F32)
        self.tb[...] = total.astype(BF16)
        self.b2, self.a2 = [], []
        for d in range(1, NY):
            to = lax.rem(y + d, NY)
            self.b2.append(
                self.send(
                    self.tb.at[to], self.rb2.at[d - 1],
                    self.b2_s.at[d - 1], self.b2_r.at[d - 1], (to * NX + x, grp),
                )
            )
        total = self.s1[y, :, 0:na, :].astype(F32)
        for d in range(1, NY):
            self.a1[d - 1].wait_recv()
            total = total + self.ra[d - 1].astype(F32)
        self.ta[...] = total.astype(BF16)
        for d in range(1, NX):
            to = lax.rem(x + d, NX)
            self.a2.append(
                self.send(
                    self.ta.at[to], self.ra2.at[d - 1],
                    self.a2_s.at[d - 1], self.a2_r.at[d - 1], (y * NX + to, grp),
                )
            )

    def last(self, i):
        band, grp, y, x, z, core = self.here
        quarter, zi, to_core = i // 4, (i // 2) % 2, i % 2
        to_z = 2 * (2 * core + quarter) + zi
        copy = pltpu.make_async_remote_copy(
            src_ref=self.f.at[quarter],
            dst_ref=self.r3.at[z],
            send_sem=self.z_s.at[i],
            recv_sem=self.z_r.at[z],
            device_id=(band, to_z * 2 + to_core),
            device_id_type=MESH,
        )
        return copy, jnp.logical_or(to_z != z, core != to_core)

    def share(self):
        band, grp, y, x, z, core = self.here
        n, na = self.count, self.na
        total = self.tb[y].astype(F32)
        for d in range(1, NY):
            self.b2[d - 1].wait_recv()
            total = total + self.rb2[d - 1].astype(F32)
        low = self.ta[x].astype(F32)
        for d in range(1, NX):
            self.a2[d - 1].wait_recv()
            low = low + self.ra2[d - 1].astype(F32)
        both = jnp.concatenate([low, total], 0)
        self.f[0] = both[0:n]
        self.f[1] = both[n : 2 * n]
        for i in range(8):
            copy, away = self.last(i)
            pl.when(away)(copy.start)

    def finish(self):
        band, grp, y, x, z, core = self.here
        own_core = z // 4
        for s in range(NZ):
            come = pltpu.make_async_remote_copy(
                src_ref=self.f.at[0],
                dst_ref=self.r3.at[s],
                send_sem=self.z_s.at[0],
                recv_sem=self.z_r.at[s],
                device_id=(band, z * 2 + 1 - core),
                device_id_type=MESH,
            )
            pl.when(jnp.logical_or(z != s, core != own_core))(come.wait_recv)

        @pl.when(core == own_core)
        def _():
            self.r3[z] = self.f[lax.rem(z // 2, 2)]

        total = self.r3[0]
        for s in range(1, NZ):
            total = total + self.r3[s]
        for i, row in enumerate(self.rows):
            at = place_of(*row)
            self.red[at : at + 1, :] = total[i : i + 1, :]

    def drain(self):
        for copy in self.a1 + self.a2 + self.b1 + self.b2:
            copy.wait_send()
        for i in range(8):
            copy, away = self.last(i)
            pl.when(away)(copy.wait_send)


def part_scratch(count, na):
    half = 2 * count
    nb = half - na
    dma = pltpu.SemaphoreType.DMA
    return [
        pltpu.VMEM((128 * count, 128), F32),
        pltpu.VMEM((NY, NX, half, 128), BF16),
        pltpu.VMEM((NY, NX, half, 128), BF16),
        pltpu.VMEM((NY, NX, half, 128), BF16),
        pltpu.VMEM((NY - 1, NX, na, 128), BF16),
        pltpu.VMEM((NX, na, 128), BF16),
        pltpu.VMEM((NX - 1, na, 128), BF16),
        pltpu.VMEM((NX - 1, NY, nb, 128), BF16),
        pltpu.VMEM((NY, nb, 128), BF16),
        pltpu.VMEM((NY - 1, nb, 128), BF16),
        pltpu.VMEM((2, count, 128), F32),
        pltpu.VMEM((NZ, count, 128), F32),
        pltpu.VMEM((count, 128), F32),
        dma((1,)), dma((1,)),
        dma((NY - 1,)), dma((NY - 1,)),
        dma((NX - 1,)), dma((NX - 1,)),
        dma((NX - 1,)), dma((NX - 1,)),
        dma((NY - 1,)), dma((NY - 1,)),
        dma((8,)), dma((NZ,)),
    ]


def kernel(
    tok_hbm, cot_hbm, oce_hbm, land_hbm, wqkv_hbm, wproj_hbm, rb_hbm,
    block_ref, grad_out_ref, red_ref,
    tok_ref, cot_ref, oce_ref, land_ref, wqkv_ref, wproj_ref, rb_ref,
    htok_ref, hcot_ref, hoce_ref, uu_ref, ug_ref, hu_ref, hg_ref,
    x_ref, c_ref, n_ref, inv_ref, mask_ref, h_ref, qkv_ref, dz_ref, do_ref, o_ref, dqkv_ref,
    p_ref, bias_ref, db_ref, grad_ref, bt_ref, load_sem, halo_s, halo_r, *rest,
):
    band = lax.axis_index("band")
    grp = lax.axis_index("grp")
    y, x = band // NX, lax.rem(band, NX)
    z, core = grp // 2, lax.rem(grp, 2)
    linear = band * 16 + grp
    after = lax.rem(linear + 1, 512)
    before = lax.rem(linear + 511, 512)
    after_id = (after // 16, lax.rem(after, 16))
    before_id = (before // 16, lax.rem(before, 16))

    loads = []
    for i, (src, dst) in enumerate(
        (
            (tok_hbm, tok_ref), (oce_hbm, oce_ref), (land_hbm, land_ref), (wqkv_hbm, wqkv_ref),
            (cot_hbm, cot_ref), (wproj_hbm, wproj_ref), (rb_hbm, rb_ref),
        )
    ):
        loads.append(pltpu.make_async_copy(src, dst, load_sem.at[i]))
        loads[-1].start()

    barrier = pltpu.get_barrier_semaphore()
    peers = [after_id, before_id]
    peers += [(band, lax.rem(grp + d, 16)) for d in range(1, 16)]
    peers += [(lax.rem(y + d, NY) * NX + x, grp) for d in range(1, NY)]
    peers += [(y * NX + lax.rem(x + d, NX), grp) for d in range(1, NX)]
    for peer in peers:
        pl.semaphore_signal(barrier, inc=1, device_id=peer, device_id_type=MESH)

    def send(src, dst, s, r, to):
        copy = pltpu.make_async_remote_copy(
            src_ref=src, dst_ref=dst, send_sem=s, recv_sem=r, device_id=to, device_id_type=MESH
        )
        copy.start()
        return copy

    loads[0].wait()
    stage_rows([tok_ref[4 + i] for i in range(4)], 0, x_ref)

    pl.semaphore_wait(barrier, len(peers))
    halos = [
        send(tok_hbm.at[pl.ds(0, 4)], htok_ref, halo_s.at[0], halo_r.at[0], before_id),
        send(oce_hbm, hoce_ref, halo_s.at[1], halo_r.at[1], before_id),
        send(cot_hbm.at[pl.ds(0, 4)], hcot_ref, halo_s.at[2], halo_r.at[2], before_id),
    ]

    def norm(i, carry):
        rows = pl.ds(pl.multiple_of(i * 64, 64), 64)
        value = x_ref[rows, :]
        centered = value - jnp.mean(value, -1, keepdims=True)
        inv = lax.rsqrt(jnp.mean(centered * centered, -1, keepdims=True) + EPS)
        n = centered * inv
        n_ref[rows, :] = n
        inv_ref[rows, :] = jnp.broadcast_to(inv, (64, 128))
        h_ref[rows, :] = n.astype(BF16)
        return carry

    def project(half):
        rows = slice(OWN * half, OWN * half + OWN)
        qkv_ref[rows, :] = dot_nn(h_ref[rows, :], wqkv_ref[...]).astype(BF16)

    def pull(half):
        rows = slice(OWN * half, OWN * half + OWN)
        wide = jnp.concatenate([mask_ref[rows, :]] * 3, 1)
        dz_ref[rows, :] = (wide * c_ref[rows, :]).astype(BF16)
        do_ref[rows, :] = dot_nt(dz_ref[rows, :], wproj_ref[...]).astype(BF16)

    lax.fori_loop(0, 3, norm, 0)
    loads[1].wait()
    loads[2].wait()
    land = land_ref[...].astype(F32)
    stage_mask(oce_ref[4:8, :].astype(F32), land, 0, mask_ref)
    loads[3].wait()
    project(0)
    loads[4].wait()
    stage_rows([cot_ref[4 + i] for i in range(4)], 0, c_ref)
    loads[5].wait()
    pull(0)
    loads[6].wait()
    for i in range(6):
        pair = jnp.concatenate([rb_ref[2 * i], rb_ref[2 * i + 1]], 0)
        bias_ref[:, 128 * i : 128 * i + 128] = pair.T
    db_ref[...] = jnp.zeros_like(db_ref)

    here_lower = jnp.broadcast_to(linear, (48, C)) < 511
    halos[0].wait_recv()
    stage_rows([jnp.where(here_lower, htok_ref[i].astype(F32), 0.0) for i in range(4)], 1, x_ref)
    lax.fori_loop(3, 6, norm, 0)
    project(1)
    halos[1].wait_recv()
    ocean = jnp.where(jnp.broadcast_to(linear, (4, 48)) < 511, hoce_ref[0:4, :].astype(F32), 0.0)
    stage_mask(ocean, land, 1, mask_ref)

    head = lax.broadcasted_iota(jnp.int32, (64, 128), 1) // 32
    picks = [(head == i).astype(F32) for i in range(4)]
    picks_low = [p.astype(BF16) for p in picks]

    def spread(a):
        return jnp.concatenate([a * p for p in picks_low], 0)

    def fold(value):
        total = value[0:64] * picks[0]
        for i in range(1, 4):
            total = total + value[64 * i : 64 * i + 64] * picks[i]
        return total

    def two(w):
        first = pl.ds(pl.multiple_of(w * 32, 32), 32)
        second = pl.ds(pl.multiple_of(OWN + w * 32, 32), 32)
        return first, second

    def load(ref, w, lanes):
        first, second = two(w)
        return jnp.concatenate([ref[first, lanes], ref[second, lanes]], 0)

    def store(ref, w, lanes, value):
        first, second = two(w)
        ref[first, lanes] = value[0:32]
        ref[second, lanes] = value[32:64]

    def lanes_of(g):
        return [slice(C * i + 128 * g, C * i + 128 * g + 128) for i in range(3)] + [
            slice(256 * g, 256 * g + 256)
        ]

    def forward(w, carry):
        whole = pl.ds(pl.multiple_of(w * 64, 64), 64)
        live = jnp.concatenate([load(mask_ref, w, slice(0, 128))] * 2, 1) > 0.5
        for g in range(HG):
            q_lanes, k_lanes, v_lanes, wide = lanes_of(g)
            q4 = spread(load(qkv_ref, w, q_lanes))
            s = dot_nt(load(qkv_ref, w, k_lanes), q4) * SCALE + bias_ref[:, wide]
            s = jnp.where(live, s, MASKED)
            weights = jnp.exp(s - jnp.max(s, 0, keepdims=True))
            p = weights * (1.0 / jnp.sum(weights, 0, keepdims=True))
            p_ref[whole, wide] = p
            store(o_ref, w, q_lanes, fold(dot_tn(p.astype(BF16), load(qkv_ref, w, v_lanes))).astype(BF16))
        return carry

    def backward(g):
        q_lanes, k_lanes, v_lanes, wide = lanes_of(g)

        def step(w, carry):
            whole = pl.ds(pl.multiple_of(w * 64, 64), 64)
            q4 = spread(load(qkv_ref, w, q_lanes))
            do4 = spread(load(do_ref, w, q_lanes))
            p = p_ref[whole, wide]
            dp = dot_nt(load(qkv_ref, w, v_lanes), do4)
            store(dqkv_ref, w, v_lanes, dot_nn(p.astype(BF16), do4).astype(BF16))
            ds = p * (dp - jnp.sum(p * dp, 0, keepdims=True))
            db_ref[:, wide] += ds
            dsc = (ds * SCALE).astype(BF16)
            store(dqkv_ref, w, k_lanes, dot_nn(dsc, q4).astype(BF16))
            dq = fold(dot_tn(dsc, load(qkv_ref, w, k_lanes)))
            store(dqkv_ref, w, q_lanes, dq.astype(BF16))
            return carry

        lax.fori_loop(0, WB, step, 0, unroll=3)
        for k in (g, 3 + g, 6 + g):
            grad_ref[k] = dot_tn(h_ref[...], dqkv_ref[:, 128 * k : 128 * k + 128])

    lax.fori_loop(0, WB, forward, 0, unroll=2)

    halos[2].wait_recv()
    stage_rows([jnp.where(here_lower, hcot_ref[i].astype(F32), 0.0) for i in range(4)], 1, c_ref)
    pull(1)

    here = (band, grp, y, x, z, core)
    parts = []
    at = 0
    for rows, count, na in PARTS:
        parts.append(Part(rows, count, na, rest[at : at + 25], here, send, (grad_ref, bt_ref), red_ref))
        at += 25
    first, second = parts

    for k in range(3):
        grad_ref[9 + k] = dot_tn(o_ref[...], dz_ref[:, 128 * k : 128 * k + 128])
    backward(0)
    first.start()
    wide_mask = jnp.concatenate([mask_ref[...]] * 3, 1)
    x_ref[...] = wide_mask * dot_nn(o_ref[...], wproj_ref[...])
    for i in range(4):
        uu_ref[i] = grid_row(x_ref, 1, i).astype(BF16)
    halo_u = send(uu_ref, hu_ref, halo_s.at[3], halo_r.at[3], after_id)
    for i in range(4):
        row = grid_row(x_ref, 0, i).astype(BF16).astype(F32)
        block_ref[4 + i] = (tok_ref[4 + i].astype(F32) + row).astype(BF16)
    first.spread()
    backward(1)
    backward(2)
    for i in range(6):
        bt_ref[128 * i : 128 * i + 128, 0:64] = db_ref[:, 128 * i : 128 * i + 128].T
    second.start()
    first.turn()

    x_ref[...] = dot_nt(dqkv_ref[...], wqkv_ref[...])
    second.spread()

    def back(i, carry):
        rows = pl.ds(pl.multiple_of(i * 64, 64), 64)
        dh = x_ref[rows, :]
        n = n_ref[rows, :]
        inv = jnp.concatenate([inv_ref[rows, :]] * 3, 1)
        slope = jnp.mean(dh * n, -1, keepdims=True)
        x_ref[rows, :] = inv * (dh - jnp.mean(dh, -1, keepdims=True) - n * slope)
        return carry

    lax.fori_loop(0, WB, back, 0)
    for i in range(4):
        ug_ref[i] = grid_row(x_ref, 1, i).astype(BF16)
    halo_g = send(ug_ref, hg_ref, halo_s.at[4], halo_r.at[4], after_id)
    first.share()
    for i in range(4):
        row = grid_row(x_ref, 0, i).astype(BF16).astype(F32)
        grad_out_ref[4 + i] = (cot_ref[4 + i].astype(F32) + row).astype(BF16)
    second.turn()
    inner = jnp.broadcast_to(linear, (4, 48, C)) > 0
    halo_u.wait_recv()
    low = jnp.where(inner, hu_ref[...].astype(F32), 0.0)
    block_ref[0:4] = (tok_ref[0:4].astype(F32) + low).astype(BF16)
    first.finish()
    second.share()
    halo_g.wait_recv()
    low = jnp.where(inner, hg_ref[...].astype(F32), 0.0)
    grad_out_ref[0:4] = (cot_ref[0:4].astype(F32) + low).astype(BF16)
    red_ref[39:40, :] = jnp.zeros((1, 128), F32)
    second.finish()
    for copy in halos + [halo_u, halo_g]:
        copy.wait_send()
    first.drain()
    second.drain()


def local(tokens, cotangent, ocean_mask, land_mask, w_qkv, w_proj, rel_bias):
    grid = jax.ShapeDtypeStruct((8, 48, C), BF16)
    dma = pltpu.SemaphoreType.DMA
    half = pltpu.VMEM((4, 48, C), BF16)
    scratch = [
        pltpu.VMEM((8, 48, C), BF16),
        pltpu.VMEM((8, 48, C), BF16),
        pltpu.VMEM((8, 48), jnp.int32),
        pltpu.VMEM((1, 6), jnp.int32),
        pltpu.VMEM((C, 3 * C), BF16),
        pltpu.VMEM((C, C), BF16),
        pltpu.VMEM((12, 64, 64), F32),
        half, half, pltpu.VMEM((8, 48), jnp.int32), half, half, half, half,
        pltpu.VMEM((C, C), F32),
        pltpu.VMEM((C, C), F32),
        pltpu.VMEM((C, C), F32),
        pltpu.VMEM((C, 128), F32),
        pltpu.VMEM((C, 128), F32),
        pltpu.VMEM((C, C), BF16),
        pltpu.VMEM((C, 3 * C), BF16),
        pltpu.VMEM((C, C), BF16),
        pltpu.VMEM((C, C), BF16),
        pltpu.VMEM((C, C), BF16),
        pltpu.VMEM((C, 3 * C), BF16),
        pltpu.VMEM((C, 768), F32),
        pltpu.VMEM((64, 768), F32),
        pltpu.VMEM((64, 768), F32),
        pltpu.VMEM((12, C, 128), F32),
        pltpu.VMEM((768, 128), F32),
        dma((7,)), dma((5,)), dma((5,)),
    ]
    for rows, count, na in PARTS:
        scratch += part_scratch(count, na)
    block_out, token_grad, red = pl.pallas_call(
        kernel,
        out_shape=[grid, grid, jax.ShapeDtypeStruct((40, 128), F32)],
        in_specs=[pl.BlockSpec(memory_space=pltpu.HBM)] * 7,
        out_specs=[pl.BlockSpec(memory_space=pltpu.VMEM)] * 3,
        scratch_shapes=scratch,
        compiler_params=pltpu.CompilerParams(
            collective_id=0, has_side_effects=True, vmem_limit_bytes=48 * 2**20
        ),
        cost_estimate=pl.CostEstimate(flops=15 * 10**8, bytes_accessed=5 * 10**6, transcendentals=300000),
        name="window_block",
    )(tokens, cotangent, ocean_mask, land_mask, w_qkv, w_proj, rel_bias)

    place = lax.rem(lax.axis_index("grp"), 4)
    outs = []
    for first, rows, size in ((0, 27, 864), (27, 9, 288), (36, 3, 96)):
        flat = red[first : first + rows].reshape(-1)
        outs.append(lax.dynamic_slice(flat, (place * size,), (size,)))
    return (block_out, token_grad, *outs)


def solution(mesh):
    split = ("band", "grp")
    placed = (
        P(split, None, None),
        P(split, None, None),
        P(split, None),
        P(split, None),
        P(),
        P(),
        P(),
    )
    return jax.shard_map(
        local,
        mesh=mesh,
        in_specs=placed,
        out_specs=(P(split, None, None), P(split, None, None), P(split), P(split), P(split)),
        check_vma=False,
    )
```

time: 380 us -> 62.2 us (0.16)
  waiting for transfers between devices: 277 us -> 0 us
  Pallas kernels: 0 us -> 52.1 us
  local copies, waits for them, and re-layouts: 37 us -> 9.06 us
  starting transfers between devices: 18.9 us -> 0 us
  matrix products: 18.4 us -> 0 us
  between operations: 14.5 us -> 0.69 us
  other arithmetic: 12.5 us -> 0 us
    unnamed x2 -> x0, waiting for transfers between devices: 277 us -> none
    pallas_call x0 -> x1, Pallas kernels: none -> 52.1 us  [local(): pl.pallas_call(kernel, out_shape=[grid, grid, jax.ShapeDtypeStruct((40, 1...]
    ppermute x5 -> x0, starting transfers between devices: 18.8 us -> none  [from_behind(): return lax.ppermute(block, axis, route)]
    reshape x7 -> x3, local copies, waits for them, and re-layouts: 15.5 us -> 0.01 us  [local(): flat = red[first:first + rows].reshape(-1)]
    dot_general x11 -> x0, matrix products: 14.2 us -> none  [the longest x1 3.1 us: window_pass(): grad_qkv = jnp.dot(hidden.T, qkv_grad, preferred_element_type=jnp.float32)]
    convert_element_type x10 -> x0, other arithmetic: 5.85 us -> none  [the longest x1 1.73 us: local(): (tokens.astype(jnp.float32) + full_update.astype(jnp.float32)).astype(jnp...]
    sub x2 -> x0, other arithmetic: 4.37 us -> none  [the longest x1 3.71 us: window_pass(): probs_grad - jnp.sum(probs * probs_grad, -1, keepdims=True)]
    sub x1 -> x0, matrix products: 4.2 us -> none  [window_pass(): weights = jnp.exp(scores - row_max)]
  transfers between devices with their start and end apart: 6 -> 0, of which waited for: 2 -> 0; matrix products, arithmetic and copies ran while one was open for 6% -> 0% of each run, Pallas kernels for 0% -> 0%
where the time goes in v1:
time: 62.2 us; the launch traced here: 61.9 us
  Pallas kernels  52.1 us (84%)
  local copies, waits for them, and re-layouts  9.06 us (15%)
  between operations  0.69 us (1%)
    pallas_call x1, Pallas kernels, local(): pl.pallas_call(kernel, out_shape=[grid, grid, jax.ShapeDtypeStruct((40, 1...  52.1 us
    unnamed x16, local copies, waits for them, and re-layouts  7.14 us
    dynamic_slice x3, local copies, waits for them, and re-layouts, local(): outs.append(lax.dynamic_slice(flat, (place * size,), (size,)))  1.91 us

profile of v1, /device:TPU:1, one launch (start us, length us, event | category | flops | bytes accessed | tf_op | source)
XLA Modules:
  0.0 61.9 jit_solution(13384007895854647933)
XLA Ops:
  0.6 0.0 copy-start.5
  0.7 0.0 copy-start.6
  0.7 0.7 %copy-done.5 = s32[8,48]{1,0:T(8,128)S(1)} copy-done((s32[8,48]{1,0:T(8,128)S(1)}, s32[8,48]{1,0:T(8,128)}, u32[]{:S(2)}) %copy-start.5) | copy-done | bytes 1560
  1.3 0.0 copy-done.6
  1.3 0.0 copy-start
  1.3 1.2 %copy-done = bf16[384,1152]{1,0:T(8,128)(2,1)S(1)} copy-done((bf16[384,1152]{1,0:T(8,128)(2,1)S(1)}, bf16[384,1152]{1,0:T(8,128)(2,1)}, u32[]{:S(2)}) %copy-start) | copy-done | bytes 884760
  2.5 0.0 copy-start.1
  2.5 1.0 %copy-done.1 = f32[12,64,64]{2,1,0:T(8,128)S(1)} copy-done((f32[12,64,64]{2,1,0:T(8,128)S(1)}, f32[12,64,64]{2,1,0:T(8,128)}, u32[]{:S(2)}) %copy-start.1) | copy-done | bytes 196632
  3.5 0.0 copy-start.2
  3.5 1.0 %copy-done.2 = bf16[8,48,384]{2,1,0:T(8,128)(2,1)S(1)} copy-done((bf16[8,48,384]{2,1,0:T(8,128)(2,1)S(1)}, bf16[8,48,384]{2,1,0:T(8,128)(2,1)}, u32[]{:S(2)}) %copy-start.2) | copy-done | bytes 294936
  4.5 0.0 copy-start.3
  4.5 1.0 %copy-done.3 = bf16[8,48,384]{2,1,0:T(8,128)(2,1)S(1)} copy-done((bf16[8,48,384]{2,1,0:T(8,128)(2,1)S(1)}, bf16[8,48,384]{2,1,0:T(8,128)(2,1)}, u32[]{:S(2)}) %copy-start.3) | copy-done | bytes 294936
  5.4 0.0 copy-start.4
  5.4 1.0 %copy-done.4 = bf16[384,384]{1,0:T(8,128)(2,1)S(1)} copy-done((bf16[384,384]{1,0:T(8,128)(2,1)S(1)}, bf16[384,384]{1,0:T(8,128)(2,1)}, u32[]{:S(2)}) %copy-start.4) | copy-done | bytes 294936
  6.4 52.1 %window_block.1 = (bf16[8,48,384]{2,1,0:T(8,128)(2,1)S(1)}, bf16[8,48,384]{2,1,0:T(8,128)(2,1)S(1)}, f32[40,128]{1,0:T(8,128)S(1)}) custom-call(bf16[8,48,384]{2,1,0:T(8,128)(2,1)S(1)} %copy-done.2, bf16[8,48,384]{2,1,0:T(8,128)(2,1)S(1)} %copy-done.3, s32[8,48]{1,0:T(8,128)S(1)} %copy-done.5, s32[1,6]{1,0:T(1,128)S(1)} %copy-done.6, ...), custom_call_target="tpu_custom_call" | custom-call | flops 1500000000 | bytes 5000000 | tf_op jit(solution)/shard_map/window_block/pallas_call | solution.py:548
  58.5 0.7 %dynamic_slice.9 = f32[864]{0:T(1024)} dynamic-slice(f32[3456]{0:T(1024)S(1)} %slice_bitcast_fusion, s32[]{:T(128)S(6)} %select_n.9), dynamic_slice_sizes={864} | dynamic-slice | bytes 6916 | tf_op jit(solution)/shard_map/dynamic_slice | solution.py:565
  59.2 0.7 %dynamic_slice.10 = f32[288]{0:T(512)} dynamic-slice(f32[1152]{0:T(1024)S(1)} %slice_bitcast_fusion.1, s32[]{:T(128)S(6)} %select_n.10), dynamic_slice_sizes={288} | dynamic-slice | bytes 2308 | tf_op jit(solution)/shard_map/dynamic_slice | solution.py:565
  59.9 0.6 dynamic_slice.11
  60.5 0.7 %copy.14 = bf16[8,48,384]{2,1,0:T(8,128)(2,1)} copy(bf16[8,48,384]{2,1,0:T(8,128)(2,1)S(1)} %get-tuple-element.16) | data formatting | bytes 589824
  61.2 0.7 %copy.15 = bf16[8,48,384]{2,1,0:T(8,128)(2,1)} copy(bf16[8,48,384]{2,1,0:T(8,128)(2,1)S(1)} %get-tuple-element.17) | data formatting | bytes 589824
  (3 shorter events, 0.0 us)
Async XLA Ops:
  0.6 0.7 %copy-start.5 = (s32[8,48]{1,0:T(8,128)S(1)}, s32[8,48]{1,0:T(8,128)}, u32[]{:S(2)}) copy-start(s32[8,48]{1,0:T(8,128)} %oce_hbm.1) | copy-start | bytes 4612
  0.7 0.7 %copy-start.6 = (s32[1,6]{1,0:T(1,128)S(1)}, s32[1,6]{1,0:T(1,128)}, u32[]{:S(2)}) copy-start(s32[1,6]{1,0:T(1,128)} %land_hbm.1) | copy-start | bytes 76
  1.3 1.2 %copy-start = (bf16[384,1152]{1,0:T(8,128)(2,1)S(1)}, bf16[384,1152]{1,0:T(8,128)(2,1)}, u32[]{:S(2)}) copy-start(bf16[384,1152]{1,0:T(8,128)(2,1)} %wqkv_hbm.1) | copy-start | bytes 2654212
  2.5 1.0 %copy-start.1 = (f32[12,64,64]{2,1,0:T(8,128)S(1)}, f32[12,64,64]{2,1,0:T(8,128)}, u32[]{:S(2)}) copy-start(f32[12,64,64]{2,1,0:T(8,128)} %rb_hbm.1) | copy-start | bytes 589828
  3.5 1.0 %copy-start.2 = (bf16[8,48,384]{2,1,0:T(8,128)(2,1)S(1)}, bf16[8,48,384]{2,1,0:T(8,128)(2,1)}, u32[]{:S(2)}) copy-start(bf16[8,48,384]{2,1,0:T(8,128)(2,1)} %tok_hbm.1) | copy-start | bytes 884740
  4.5 1.0 %copy-start.3 = (bf16[8,48,384]{2,1,0:T(8,128)(2,1)S(1)}, bf16[8,48,384]{2,1,0:T(8,128)(2,1)}, u32[]{:S(2)}) copy-start(bf16[8,48,384]{2,1,0:T(8,128)(2,1)} %cot_hbm.1) | copy-start | bytes 884740
  5.4 1.0 %copy-start.4 = (bf16[384,384]{1,0:T(8,128)(2,1)S(1)}, bf16[384,384]{1,0:T(8,128)(2,1)}, u32[]{:S(2)}) copy-start(bf16[384,384]{1,0:T(8,128)(2,1)} %wproj_hbm.1) | copy-start | bytes 884740

commit v2 on v1

--- a/solution.py
+++ b/solution.py
@@ -19,6 +19,7 @@
 
 NY, NX, NZ = 8, 4, 8
 OWN = 192
+VMEM_BYTES = 62 * 2**20
 
 
 def qkv_rows(g):
@@ -33,8 +34,20 @@
 ]
 
 
-def place_of(kind, j, k):
-    return {"qkv": 9 * j + k, "proj": 27 + 3 * j + k, "bias": 36 + j}[kind]
+def owned(g):
+    qkv = [min(27 * g // 4 + i, 26) for i in range(8)]
+    proj = [min(9 * g // 4 + i, 8) for i in range(3)]
+    bias = [min(3 * g // 4 + i, 2) for i in range(2)]
+    return (
+        [("qkv", r // 9, r % 9) for r in qkv]
+        + [("proj", r // 3, r % 3) for r in proj]
+        + [("bias", r, 0) for r in bias]
+    )
+
+
+def carried(rows, g):
+    need = owned(g)
+    return [i for i, row in enumerate(rows) if row in need]
 
 
 def dot_nt(a, b):
@@ -79,7 +92,7 @@
     def __init__(self, rows, count, along_y, refs, here, send, sources, red_ref):
         (
             self.pk, self.pack, self.r0, self.s1, self.ra, self.ta, self.ra2, self.rb, self.tb, self.rb2,
-            self.f, self.r3, self.tot, self.core_s, self.core_r, self.a1_s, self.a1_r, self.a2_s, self.a2_r,
+            self.f, self.r3, self.core_s, self.core_r, self.a1_s, self.a1_r, self.a2_s, self.a2_r,
             self.b1_s, self.b1_r, self.b2_s, self.b2_r, self.z_s, self.z_r,
         ) = refs
         self.rows, self.count, self.na = rows, count, along_y
@@ -113,6 +126,8 @@
             return carry
 
         lax.fori_loop(0, NY, narrow, 0)
+        for i in range(8):
+            self.f[i] = jnp.zeros((8, 128), F32)
         self.core_copy = self.send(
             self.pack, self.r0, self.core_s.at[0], self.core_r.at[0], (band, z * 2 + 1 - core)
         )
@@ -185,7 +200,7 @@
         quarter, zi, to_core = i // 4, (i // 2) % 2, i % 2
         to_z = 2 * (2 * core + quarter) + zi
         copy = pltpu.make_async_remote_copy(
-            src_ref=self.f.at[quarter],
+            src_ref=self.f.at[i],
             dst_ref=self.r3.at[z],
             send_sem=self.z_s.at[i],
             recv_sem=self.z_r.at[z],
@@ -206,8 +221,10 @@
             self.a2[d - 1].wait_recv()
             low = low + self.ra2[d - 1].astype(F32)
         both = jnp.concatenate([low, total], 0)
-        self.f[0] = both[0:n]
-        self.f[1] = both[n : 2 * n]
+        for i in range(8):
+            for at, row in enumerate(carried(self.rows, i % 4)):
+                first = n * (i // 4) + row
+                self.f[i, at : at + 1, :] = both[first : first + 1, :]
         for i in range(8):
             copy, away = self.last(i)
             pl.when(away)(copy.start)
@@ -228,14 +245,20 @@
 
         @pl.when(core == own_core)
         def _():
-            self.r3[z] = self.f[lax.rem(z // 2, 2)]
+            self.r3[z] = self.f[4 * lax.rem(z // 2, 2) + lax.rem(grp, 4)]
 
         total = self.r3[0]
         for s in range(1, NZ):
             total = total + self.r3[s]
-        for i, row in enumerate(self.rows):
-            at = place_of(*row)
-            self.red[at : at + 1, :] = total[i : i + 1, :]
+        for g in range(4):
+            kept = [self.rows[i] for i in carried(self.rows, g)]
+
+            @pl.when(lax.rem(grp, 4) == g)
+            def _(g=g, kept=kept):
+                for at, row in enumerate(owned(g)):
+                    if row in kept:
+                        i = kept.index(row)
+                        self.red[at : at + 1, :] = total[i : i + 1, :]
 
     def drain(self):
         for copy in self.a1 + self.a2 + self.b1 + self.b2:
@@ -260,9 +283,8 @@
         pltpu.VMEM((NX - 1, NY, nb, 128), BF16),
         pltpu.VMEM((NY, nb, 128), BF16),
         pltpu.VMEM((NY - 1, nb, 128), BF16),
-        pltpu.VMEM((2, count, 128), F32),
-        pltpu.VMEM((NZ, count, 128), F32),
-        pltpu.VMEM((count, 128), F32),
+        pltpu.VMEM((8, 8, 128), F32),
+        pltpu.VMEM((NZ, 8, 128), F32),
         dma((1,)), dma((1,)),
         dma((NY - 1,)), dma((NY - 1,)),
         dma((NX - 1,)), dma((NX - 1,)),
@@ -274,11 +296,12 @@
 
 def kernel(
     tok_hbm, cot_hbm, oce_hbm, land_hbm, wqkv_hbm, wproj_hbm, rb_hbm,
+    block_hbm, grad_hbm, red_hbm,
     block_ref, grad_out_ref, red_ref,
     tok_ref, cot_ref, oce_ref, land_ref, wqkv_ref, wproj_ref, rb_ref,
     htok_ref, hcot_ref, hoce_ref, uu_ref, ug_ref, hu_ref, hg_ref,
     x_ref, c_ref, n_ref, inv_ref, mask_ref, h_ref, qkv_ref, dz_ref, do_ref, o_ref, dqkv_ref,
-    p_ref, bias_ref, db_ref, grad_ref, bt_ref, load_sem, halo_s, halo_r, *rest,
+    p_ref, bias_ref, db_ref, grad_ref, bt_ref, load_sem, store_sem, halo_s, halo_r, *rest,
 ):
     band = lax.axis_index("band")
     grp = lax.axis_index("grp")
@@ -314,6 +337,12 @@
         )
         copy.start()
         return copy
+
+    kept = []
+
+    def keep(src, dst):
+        kept.append(pltpu.make_async_copy(src, dst, store_sem.at[len(kept)]))
+        kept[-1].start()
 
     loads[0].wait()
     stage_rows([tok_ref[4 + i] for i in range(4)], 0, x_ref)
@@ -450,66 +479,111 @@
     parts = []
     at = 0
     for rows, count, na in PARTS:
-        parts.append(Part(rows, count, na, rest[at : at + 25], here, send, (grad_ref, bt_ref), red_ref))
-        at += 25
+        parts.append(Part(rows, count, na, rest[at : at + 24], here, send, (grad_ref, bt_ref), red_ref))
+        at += 24
     first, second = parts
 
     for k in range(3):
         grad_ref[9 + k] = dot_tn(o_ref[...], dz_ref[:, 128 * k : 128 * k + 128])
     backward(0)
     first.start()
-    wide_mask = jnp.concatenate([mask_ref[...]] * 3, 1)
-    x_ref[...] = wide_mask * dot_nn(o_ref[...], wproj_ref[...])
-    for i in range(4):
-        uu_ref[i] = grid_row(x_ref, 1, i).astype(BF16)
-    halo_u = send(uu_ref, hu_ref, halo_s.at[3], halo_r.at[3], after_id)
-    for i in range(4):
-        row = grid_row(x_ref, 0, i).astype(BF16).astype(F32)
-        block_ref[4 + i] = (tok_ref[4 + i].astype(F32) + row).astype(BF16)
+    backward(1)
     first.spread()
-    backward(1)
     backward(2)
     for i in range(6):
         bt_ref[128 * i : 128 * i + 128, 0:64] = db_ref[:, 128 * i : 128 * i + 128].T
     second.start()
     first.turn()
 
-    x_ref[...] = dot_nt(dqkv_ref[...], wqkv_ref[...])
+    wide_mask = jnp.concatenate([mask_ref[...]] * 3, 1)
+    x_ref[...] = wide_mask * dot_nn(o_ref[...], wproj_ref[...])
+    for i in range(4):
+        uu_ref[i] = grid_row(x_ref, 1, i).astype(BF16)
     second.spread()
+    halo_u = send(uu_ref, hu_ref, halo_s.at[3], halo_r.at[3], after_id)
+    c_ref[...] = dot_nt(dqkv_ref[...], wqkv_ref[...])
 
     def back(i, carry):
         rows = pl.ds(pl.multiple_of(i * 64, 64), 64)
-        dh = x_ref[rows, :]
+        dh = c_ref[rows, :]
         n = n_ref[rows, :]
         inv = jnp.concatenate([inv_ref[rows, :]] * 3, 1)
         slope = jnp.mean(dh * n, -1, keepdims=True)
-        x_ref[rows, :] = inv * (dh - jnp.mean(dh, -1, keepdims=True) - n * slope)
+        c_ref[rows, :] = inv * (dh - jnp.mean(dh, -1, keepdims=True) - n * slope)
         return carry
 
     lax.fori_loop(0, WB, back, 0)
     for i in range(4):
-        ug_ref[i] = grid_row(x_ref, 1, i).astype(BF16)
+        ug_ref[i] = grid_row(c_ref, 1, i).astype(BF16)
     halo_g = send(ug_ref, hg_ref, halo_s.at[4], halo_r.at[4], after_id)
     first.share()
+    second.turn()
     for i in range(4):
         row = grid_row(x_ref, 0, i).astype(BF16).astype(F32)
+        block_ref[4 + i] = (tok_ref[4 + i].astype(F32) + row).astype(BF16)
+        row = grid_row(c_ref, 0, i).astype(BF16).astype(F32)
         grad_out_ref[4 + i] = (cot_ref[4 + i].astype(F32) + row).astype(BF16)
-    second.turn()
+    upper, lower = pl.ds(4, 4), pl.ds(0, 4)
+    keep(block_ref.at[upper], block_hbm.at[upper])
+    keep(grad_out_ref.at[upper], grad_hbm.at[upper])
+    second.share()
     inner = jnp.broadcast_to(linear, (4, 48, C)) > 0
     halo_u.wait_recv()
     low = jnp.where(inner, hu_ref[...].astype(F32), 0.0)
     block_ref[0:4] = (tok_ref[0:4].astype(F32) + low).astype(BF16)
-    first.finish()
-    second.share()
+    keep(block_ref.at[lower], block_hbm.at[lower])
     halo_g.wait_recv()
     low = jnp.where(inner, hg_ref[...].astype(F32), 0.0)
     grad_out_ref[0:4] = (cot_ref[0:4].astype(F32) + low).astype(BF16)
-    red_ref[39:40, :] = jnp.zeros((1, 128), F32)
+    keep(grad_out_ref.at[lower], grad_hbm.at[lower])
+    first.finish()
+    red_ref[13:16, :] = jnp.zeros((3, 128), F32)
     second.finish()
+    keep(red_ref, red_hbm)
     for copy in halos + [halo_u, halo_g]:
         copy.wait_send()
     first.drain()
     second.drain()
+    for copy in kept:
+        copy.wait()
+
+
+def place_kernel(
+    block_ref, grad_ref, red_hbm, block_out, grad_out, qkv_out, proj_out, bias_out, red_ref, sem
+):
+    load = pltpu.make_async_copy(red_hbm, red_ref, sem.at[2])
+    load.start()
+    copies = [
+        pltpu.make_async_copy(block_ref, block_out, sem.at[0]),
+        pltpu.make_async_copy(grad_ref, grad_out, sem.at[1]),
+    ]
+    for copy in copies:
+        copy.start()
+    g = lax.rem(lax.axis_index("grp"), 4)
+    lane = lax.broadcasted_iota(jnp.int32, (16, 128), 1)
+    load.wait()
+    red = red_ref[...]
+    following = jnp.concatenate([red[1:16], red[0:1]], 0)
+    rolled = [red]
+    for quarter in range(1, 4):
+        shift = 128 - 32 * quarter
+        value = jnp.where(lane < shift, pltpu.roll(red, shift, 1), pltpu.roll(following, shift, 1))
+        rolled.append(value)
+
+    def pick(step):
+        which = jnp.broadcast_to(lax.rem(step * g, 4), (16, 128))
+        value = rolled[0]
+        for quarter in range(1, 4):
+            value = jnp.where(which == quarter, rolled[quarter], value)
+        return value
+
+    for out, step, first, size in ((qkv_out, 27, 0, 864), (proj_out, 9, 8, 288), (bias_out, 3, 11, 96)):
+        value = pick(step)
+        for i in range(-(-size // 128)):
+            n = min(128, size - 128 * i)
+            out[pl.ds(128 * i, n)] = value[first + i, 0:n]
+    for copy in copies:
+        copy.wait()
 
 
 def local(tokens, cotangent, ocean_mask, land_mask, w_qkv, w_proj, rel_bias):
@@ -517,6 +591,9 @@
     dma = pltpu.SemaphoreType.DMA
     half = pltpu.VMEM((4, 48, C), BF16)
     scratch = [
+        pltpu.VMEM((8, 48, C), BF16),
+        pltpu.VMEM((8, 48, C), BF16),
+        pltpu.VMEM((16, 128), F32),
         pltpu.VMEM((8, 48, C), BF16),
         pltpu.VMEM((8, 48, C), BF16),
         pltpu.VMEM((8, 48), jnp.int32),
@@ -541,29 +618,37 @@
         pltpu.VMEM((64, 768), F32),
         pltpu.VMEM((12, C, 128), F32),
         pltpu.VMEM((768, 128), F32),
-        dma((7,)), dma((5,)), dma((5,)),
+        dma((7,)), dma((5,)), dma((5,)), dma((5,)),
     ]
     for rows, count, na in PARTS:
         scratch += part_scratch(count, na)
     block_out, token_grad, red = pl.pallas_call(
         kernel,
-        out_shape=[grid, grid, jax.ShapeDtypeStruct((40, 128), F32)],
+        out_shape=[grid, grid, jax.ShapeDtypeStruct((16, 128), F32)],
         in_specs=[pl.BlockSpec(memory_space=pltpu.HBM)] * 7,
-        out_specs=[pl.BlockSpec(memory_space=pltpu.VMEM)] * 3,
+        out_specs=[pl.BlockSpec(memory_space=pltpu.HBM)] * 3,
         scratch_shapes=scratch,
         compiler_params=pltpu.CompilerParams(
-            collective_id=0, has_side_effects=True, vmem_limit_bytes=48 * 2**20
+            collective_id=0, has_side_effects=True, vmem_limit_bytes=VMEM_BYTES
         ),
         cost_estimate=pl.CostEstimate(flops=15 * 10**8, bytes_accessed=5 * 10**6, transcendentals=300000),
         name="window_block",
     )(tokens, cotangent, ocean_mask, land_mask, w_qkv, w_proj, rel_bias)
 
-    place = lax.rem(lax.axis_index("grp"), 4)
-    outs = []
-    for first, rows, size in ((0, 27, 864), (27, 9, 288), (36, 3, 96)):
-        flat = red[first : first + rows].reshape(-1)
-        outs.append(lax.dynamic_slice(flat, (place * size,), (size,)))
-    return (block_out, token_grad, *outs)
+    whole = pl.BlockSpec(memory_space=pltpu.VMEM)
+    hbm = pl.BlockSpec(memory_space=pltpu.HBM)
+    return tuple(
+        pl.pallas_call(
+            place_kernel,
+            out_shape=[grid, grid] + [jax.ShapeDtypeStruct((n,), F32) for n in (864, 288, 96)],
+            in_specs=[hbm] * 3,
+            out_specs=[hbm, hbm, whole, whole, whole],
+            scratch_shapes=[pltpu.VMEM((16, 128), F32), dma((3,))],
+            compiler_params=pltpu.CompilerParams(vmem_limit_bytes=VMEM_BYTES),
+            cost_estimate=pl.CostEstimate(flops=10**4, bytes_accessed=12 * 10**5, transcendentals=0),
+            name="outputs",
+        )(block_out, token_grad, red)
+    )
 
 
 def solution(mesh):

time: 62.2 us -> 72.3 us (1.16)
  Pallas kernels: 52.1 us -> 71.5 us
  local copies, waits for them, and re-layouts: 9.06 us -> 0 us
    pallas_call x1 -> x2, Pallas kernels: 52.1 us -> 71.5 us  [the longest x1 51.9 us: local(): pl.pallas_call(kernel, out_shape=[grid, grid, jax.ShapeDtypeStruct((16, 1...]
    unnamed x16 -> x0, local copies, waits for them, and re-layouts: 7.14 us -> none
    dynamic_slice x3 -> x0, local copies, waits for them, and re-layouts: 1.91 us -> none  [local(): outs.append(lax.dynamic_slice(flat, (place * size,), (size,)))]
where the time goes in v2:
time: 72.3 us; the launch traced here: 72.2 us
  Pallas kernels  71.5 us (99%)
    pallas_call x1, Pallas kernels, local(): pl.pallas_call(kernel, out_shape=[grid, grid, jax.ShapeDtypeStruct((16, 1...  51.9 us
    pallas_call x1, Pallas kernels, local(): pl.pallas_call(place_kernel, out_shape=[grid, grid] + [jax.ShapeDtypeStru...  19.6 us

profile of v2, /device:TPU:1, one launch (start us, length us, event | category | flops | bytes accessed | tf_op | source)
XLA Modules:
  0.0 72.2 jit_solution(10778581043285206447)
XLA Ops:
  0.6 51.9 %window_block.1 = (bf16[8,48,384]{2,1,0:T(8,128)(2,1)}, bf16[8,48,384]{2,1,0:T(8,128)(2,1)}, f32[16,128]{1,0:T(8,128)}) custom-call(bf16[8,48,384]{2,1,0:T(8,128)(2,1)} %tok_hbm.1, bf16[8,48,384]{2,1,0:T(8,128)(2,1)} %cot_hbm.1, s32[8,48]{1,0:T(8,128)} %oce_hbm.1, s32[1,6]{1,0:T(1,128)} %land_hbm.1, bf16[384,1152]{1,0:T(8,128)(2,1)} %wqkv_hbm.1, ...), custom_call_target="tpu_custom_call" | custom-call | flops 1500000000 | bytes 5000000 | tf_op jit(solution)/shard_map/window_block/pallas_call | solution.py:625
  52.6 19.6 %outputs.1 = (bf16[8,48,384]{2,1,0:T(8,128)(2,1)}, bf16[8,48,384]{2,1,0:T(8,128)(2,1)}, f32[864]{0:T(1024)}, f32[288]{0:T(512)}, f32[96]{0:T(128)}) custom-call(bf16[8,48,384]{2,1,0:T(8,128)(2,1)} %get-tuple-element.8.block_ref, bf16[8,48,384]{2,1,0:T(8,128)(2,1)} %get-tuple-element.9.grad_ref, f32[16,128]{1,0:T(8,128)} %get-tuple-element.10.red_hbm), custom_call_target="tpu_custom_call" | custom-call | flops 10000 | bytes 1200000 | tf_op jit(solution)/shard_map/outputs/pallas_call | solution.py:641

commit v3 on v2

--- a/solution.py
+++ b/solution.py
@@ -300,7 +300,7 @@
     block_ref, grad_out_ref, red_ref,
     tok_ref, cot_ref, oce_ref, land_ref, wqkv_ref, wproj_ref, rb_ref,
     htok_ref, hcot_ref, hoce_ref, uu_ref, ug_ref, hu_ref, hg_ref,
-    x_ref, c_ref, n_ref, inv_ref, mask_ref, h_ref, qkv_ref, dz_ref, do_ref, o_ref, dqkv_ref,
+    x_ref, c_ref, n_ref, inv_ref, mask_ref, h_ref, ht_ref, qkv_ref, dz_ref, do_ref, o_ref, dqkv_ref,
     p_ref, bias_ref, db_ref, grad_ref, bt_ref, load_sem, store_sem, halo_s, halo_r, *rest,
 ):
     band = lax.axis_index("band")
@@ -375,7 +375,7 @@
         dz_ref[rows, :] = (wide * c_ref[rows, :]).astype(BF16)
         do_ref[rows, :] = dot_nt(dz_ref[rows, :], wproj_ref[...]).astype(BF16)
 
-    lax.fori_loop(0, 3, norm, 0)
+    lax.fori_loop(0, 3, norm, 0, unroll=3)
     loads[1].wait()
     loads[2].wait()
     land = land_ref[...].astype(F32)
@@ -395,8 +395,9 @@
     here_lower = jnp.broadcast_to(linear, (48, C)) < 511
     halos[0].wait_recv()
     stage_rows([jnp.where(here_lower, htok_ref[i].astype(F32), 0.0) for i in range(4)], 1, x_ref)
-    lax.fori_loop(3, 6, norm, 0)
+    lax.fori_loop(3, 6, norm, 0, unroll=3)
     project(1)
+    ht_ref[...] = h_ref[...].T
     halos[1].wait_recv()
     ocean = jnp.where(jnp.broadcast_to(linear, (4, 48)) < 511, hoce_ref[0:4, :].astype(F32), 0.0)
     stage_mask(ocean, land, 1, mask_ref)
@@ -465,9 +466,9 @@
             store(dqkv_ref, w, q_lanes, dq.astype(BF16))
             return carry
 
-        lax.fori_loop(0, WB, step, 0, unroll=3)
+        lax.fori_loop(0, WB, step, 0, unroll=6)
         for k in (g, 3 + g, 6 + g):
-            grad_ref[k] = dot_tn(h_ref[...], dqkv_ref[:, 128 * k : 128 * k + 128])
+            grad_ref[k] = dot_nn(ht_ref[...], dqkv_ref[:, 128 * k : 128 * k + 128])
 
     lax.fori_loop(0, WB, forward, 0, unroll=2)
 
@@ -483,8 +484,9 @@
         at += 24
     first, second = parts
 
+    proj = dot_tn(o_ref[...], dz_ref[...])
     for k in range(3):
-        grad_ref[9 + k] = dot_tn(o_ref[...], dz_ref[:, 128 * k : 128 * k + 128])
+        grad_ref[9 + k] = proj[:, 128 * k : 128 * k + 128]
     backward(0)
     first.start()
     backward(1)
@@ -512,7 +514,7 @@
         c_ref[rows, :] = inv * (dh - jnp.mean(dh, -1, keepdims=True) - n * slope)
         return carry
 
-    lax.fori_loop(0, WB, back, 0)
+    lax.fori_loop(0, WB, back, 0, unroll=3)
     for i in range(4):
         ug_ref[i] = grid_row(c_ref, 1, i).astype(BF16)
     halo_g = send(ug_ref, hg_ref, halo_s.at[4], halo_r.at[4], after_id)
@@ -549,19 +551,24 @@
 
 
 def place_kernel(
-    block_ref, grad_ref, red_hbm, block_out, grad_out, qkv_out, proj_out, bias_out, red_ref, sem
+    block_hbm, grad_hbm, red_hbm, block_out, grad_out, qkv_out, proj_out, bias_out,
+    block_ref, grad_ref, red_ref, in_sem, out_sem,
 ):
-    load = pltpu.make_async_copy(red_hbm, red_ref, sem.at[2])
+    load = pltpu.make_async_copy(red_hbm, red_ref, in_sem.at[4])
     load.start()
-    copies = [
-        pltpu.make_async_copy(block_ref, block_out, sem.at[0]),
-        pltpu.make_async_copy(grad_ref, grad_out, sem.at[1]),
-    ]
-    for copy in copies:
-        copy.start()
+    moves = []
+    for i, (src, via, dst) in enumerate(((block_hbm, block_ref, block_out), (grad_hbm, grad_ref, grad_out))):
+        for j in range(2):
+            part = pl.ds(4 * j, 4)
+            into = pltpu.make_async_copy(src.at[part], via.at[part], in_sem.at[2 * i + j])
+            into.start()
+            moves.append((into, pltpu.make_async_copy(via.at[part], dst.at[part], out_sem.at[2 * i + j])))
+    load.wait()
+    for into, out in moves:
+        into.wait()
+        out.start()
     g = lax.rem(lax.axis_index("grp"), 4)
     lane = lax.broadcasted_iota(jnp.int32, (16, 128), 1)
-    load.wait()
     red = red_ref[...]
     following = jnp.concatenate([red[1:16], red[0:1]], 0)
     rolled = [red]
@@ -582,8 +589,8 @@
         for i in range(-(-size // 128)):
             n = min(128, size - 128 * i)
             out[pl.ds(128 * i, n)] = value[first + i, 0:n]
-    for copy in copies:
-        copy.wait()
+    for into, out in moves:
+        out.wait()
 
 
 def local(tokens, cotangent, ocean_mask, land_mask, w_qkv, w_proj, rel_bias):
@@ -607,6 +614,7 @@
         pltpu.VMEM((C, C), F32),
         pltpu.VMEM((C, 128), F32),
         pltpu.VMEM((C, 128), F32),
+        pltpu.VMEM((C, C), BF16),
         pltpu.VMEM((C, C), BF16),
         pltpu.VMEM((C, 3 * C), BF16),
         pltpu.VMEM((C, C), BF16),
@@ -643,7 +651,13 @@
             out_shape=[grid, grid] + [jax.ShapeDtypeStruct((n,), F32) for n in (864, 288, 96)],
             in_specs=[hbm] * 3,
             out_specs=[hbm, hbm, whole, whole, whole],
-            scratch_shapes=[pltpu.VMEM((16, 128), F32), dma((3,))],
+            scratch_shapes=[
+                pltpu.VMEM((8, 48, C), BF16),
+                pltpu.VMEM((8, 48, C), BF16),
+                pltpu.VMEM((16, 128), F32),
+                dma((5,)),
+                dma((4,)),
+            ],
             compiler_params=pltpu.CompilerParams(vmem_limit_bytes=VMEM_BYTES),
             cost_estimate=pl.CostEstimate(flops=10**4, bytes_accessed=12 * 10**5, transcendentals=0),
             name="outputs",

time: 72.3 us -> 54.4 us (0.75)
  Pallas kernels: 71.5 us -> 53.6 us
    pallas_call x1, Pallas kernels: 19.6 us -> 2.46 us  [local(): pl.pallas_call(place_kernel, out_shape=[grid, grid] + [jax.ShapeDtypeStru...]
    pallas_call x1, Pallas kernels: 51.9 us -> 51.2 us  [local(): pl.pallas_call(kernel, out_shape=[grid, grid, jax.ShapeDtypeStruct((16, 1...]
where the time goes in v3:
time: 54.4 us; the launch traced here: 54.3 us
  Pallas kernels  53.6 us (99%)
  between operations  0.64 us (1%)
    pallas_call x1, Pallas kernels, local(): pl.pallas_call(kernel, out_shape=[grid, grid, jax.ShapeDtypeStruct((16, 1...  51.2 us
    pallas_call x1, Pallas kernels, local(): pl.pallas_call(place_kernel, out_shape=[grid, grid] + [jax.ShapeDtypeStru...  2.46 us

profile of v3, /device:TPU:1, one launch (start us, length us, event | category | flops | bytes accessed | tf_op | source)
XLA Modules:
  0.0 54.3 jit_solution(13842043398549032750)
XLA Ops:
  0.6 51.2 %window_block.1 = (bf16[8,48,384]{2,1,0:T(8,128)(2,1)}, bf16[8,48,384]{2,1,0:T(8,128)(2,1)}, f32[16,128]{1,0:T(8,128)}) custom-call(bf16[8,48,384]{2,1,0:T(8,128)(2,1)} %tok_hbm.1, bf16[8,48,384]{2,1,0:T(8,128)(2,1)} %cot_hbm.1, s32[8,48]{1,0:T(8,128)} %oce_hbm.1, s32[1,6]{1,0:T(1,128)} %land_hbm.1, bf16[384,1152]{1,0:T(8,128)(2,1)} %wqkv_hbm.1, ...), custom_call_target="tpu_custom_call" | custom-call | flops 1500000000 | bytes 5000000 | tf_op jit(solution)/shard_map/window_block/pallas_call | solution.py:633
  51.8 2.5 %outputs.1 = (bf16[8,48,384]{2,1,0:T(8,128)(2,1)}, bf16[8,48,384]{2,1,0:T(8,128)(2,1)}, f32[864]{0:T(1024)}, f32[288]{0:T(512)}, f32[96]{0:T(128)}) custom-call(bf16[8,48,384]{2,1,0:T(8,128)(2,1)} %get-tuple-element.8.block_hbm, bf16[8,48,384]{2,1,0:T(8,128)(2,1)} %get-tuple-element.9.grad_hbm, f32[16,128]{1,0:T(8,128)} %get-tuple-element.10.red_hbm), custom_call_target="tpu_custom_call" | custom-call | flops 10000 | bytes 1200000 | tf_op jit(solution)/shard_map/outputs/pallas_call | solution.py:649

commit v4 on v3

--- a/solution.py
+++ b/solution.py
@@ -30,8 +30,10 @@
 BIAS_ROWS = [("bias", j, 0) for j in range(3)]
 PARTS = [
     (qkv_rows(0) + PROJ_ROWS[:7], 16, 16),
-    (qkv_rows(1) + qkv_rows(2) + PROJ_ROWS[7:] + BIAS_ROWS, 24, 16),
+    (qkv_rows(1)[:8], 8, 0),
+    (qkv_rows(1)[8:] + qkv_rows(2) + PROJ_ROWS[7:] + BIAS_ROWS, 16, 16),
 ]
+SLOTS = 13
 
 
 def owned(g):
@@ -43,11 +45,6 @@
         + [("proj", r // 3, r % 3) for r in proj]
         + [("bias", r, 0) for r in bias]
     )
-
-
-def carried(rows, g):
-    need = owned(g)
-    return [i for i, row in enumerate(rows) if row in need]
 
 
 def dot_nt(a, b):
@@ -89,17 +86,17 @@
 
 
 class Part:
-    def __init__(self, rows, count, along_y, refs, here, send, sources, red_ref):
+    def __init__(self, rows, count, along_y, refs, here, send, sources):
         (
             self.pk, self.pack, self.r0, self.s1, self.ra, self.ta, self.ra2, self.rb, self.tb, self.rb2,
-            self.f, self.r3, self.core_s, self.core_r, self.a1_s, self.a1_r, self.a2_s, self.a2_r,
-            self.b1_s, self.b1_r, self.b2_s, self.b2_r, self.z_s, self.z_r,
+            self.core_s, self.core_r, self.a1_s, self.a1_r, self.a2_s, self.a2_r,
+            self.b1_s, self.b1_r, self.b2_s, self.b2_r,
         ) = refs
         self.rows, self.count, self.na = rows, count, along_y
         self.half = 2 * count
         self.nb = self.half - along_y
-        self.here, self.send, self.sources, self.red = here, send, sources, red_ref
-        self.sent = []
+        self.here, self.send, self.sources = here, send, sources
+        self.a1, self.a2, self.b1, self.b2 = [], [], [], []
 
     def start(self):
         band, grp, y, x, z, core = self.here
@@ -126,8 +123,6 @@
             return carry
 
         lax.fori_loop(0, NY, narrow, 0)
-        for i in range(8):
-            self.f[i] = jnp.zeros((8, 128), F32)
         self.core_copy = self.send(
             self.pack, self.r0, self.core_s.at[0], self.core_r.at[0], (band, z * 2 + 1 - core)
         )
@@ -146,7 +141,6 @@
             return carry
 
         lax.fori_loop(0, NY, add, 0)
-        self.b1, self.a1 = [], []
         for d in range(1, NX):
             to = lax.rem(x + d, NX)
             self.b1.append(
@@ -155,7 +149,7 @@
                     self.b1_s.at[d - 1], self.b1_r.at[d - 1], (y * NX + to, grp),
                 )
             )
-        for d in range(1, NY):
+        for d in range(1, NY if na else 1):
             to = lax.rem(y + d, NY)
             self.a1.append(
                 self.send(
@@ -172,7 +166,6 @@
             self.b1[d - 1].wait_recv()
             total = total + self.rb[d - 1].astype(F32)
         self.tb[...] = total.astype(BF16)
-        self.b2, self.a2 = [], []
         for d in range(1, NY):
             to = lax.rem(y + d, NY)
             self.b2.append(
@@ -181,6 +174,8 @@
                     self.b2_s.at[d - 1], self.b2_r.at[d - 1], (to * NX + x, grp),
                 )
             )
+        if not na:
+            return
         total = self.s1[y, :, 0:na, :].astype(F32)
         for d in range(1, NY):
             self.a1[d - 1].wait_recv()
@@ -195,6 +190,34 @@
                 )
             )
 
+    def collect(self, f_ref):
+        band, grp, y, x, z, core = self.here
+        n, na = self.count, self.na
+        total = self.tb[y].astype(F32)
+        for d in range(1, NY):
+            self.b2[d - 1].wait_recv()
+            total = total + self.rb2[d - 1].astype(F32)
+        if na:
+            low = self.ta[x].astype(F32)
+            for d in range(1, NX):
+                self.a2[d - 1].wait_recv()
+                low = low + self.ra2[d - 1].astype(F32)
+            total = jnp.concatenate([low, total], 0)
+        for i in range(8):
+            for at, row in enumerate(owned(i % 4)):
+                if row in self.rows:
+                    first = n * (i // 4) + self.rows.index(row)
+                    f_ref[i, at : at + 1, :] = total[first : first + 1, :]
+
+    def drain(self):
+        for copy in self.a1 + self.a2 + self.b1 + self.b2:
+            copy.wait_send()
+
+
+class Share:
+    def __init__(self, f_ref, r3_ref, z_s, z_r, here):
+        self.f, self.r3, self.z_s, self.z_r, self.here = f_ref, r3_ref, z_s, z_r, here
+
     def last(self, i):
         band, grp, y, x, z, core = self.here
         quarter, zi, to_core = i // 4, (i // 2) % 2, i % 2
@@ -209,29 +232,19 @@
         )
         return copy, jnp.logical_or(to_z != z, core != to_core)
 
-    def share(self):
-        band, grp, y, x, z, core = self.here
-        n, na = self.count, self.na
-        total = self.tb[y].astype(F32)
-        for d in range(1, NY):
-            self.b2[d - 1].wait_recv()
-            total = total + self.rb2[d - 1].astype(F32)
-        low = self.ta[x].astype(F32)
-        for d in range(1, NX):
-            self.a2[d - 1].wait_recv()
-            low = low + self.ra2[d - 1].astype(F32)
-        both = jnp.concatenate([low, total], 0)
-        for i in range(8):
-            for at, row in enumerate(carried(self.rows, i % 4)):
-                first = n * (i // 4) + row
-                self.f[i, at : at + 1, :] = both[first : first + 1, :]
+    def start(self):
         for i in range(8):
             copy, away = self.last(i)
             pl.when(away)(copy.start)
 
-    def finish(self):
+    def finish(self, red_ref):
         band, grp, y, x, z, core = self.here
         own_core = z // 4
+
+        @pl.when(core == own_core)
+        def _():
+            self.r3[z] = self.f[4 * lax.rem(z // 2, 2) + lax.rem(grp, 4)]
+
         for s in range(NZ):
             come = pltpu.make_async_remote_copy(
                 src_ref=self.f.at[0],
@@ -242,27 +255,12 @@
                 device_id_type=MESH,
             )
             pl.when(jnp.logical_or(z != s, core != own_core))(come.wait_recv)
-
-        @pl.when(core == own_core)
-        def _():
-            self.r3[z] = self.f[4 * lax.rem(z // 2, 2) + lax.rem(grp, 4)]
-
         total = self.r3[0]
         for s in range(1, NZ):
             total = total + self.r3[s]
-        for g in range(4):
-            kept = [self.rows[i] for i in carried(self.rows, g)]
-
-            @pl.when(lax.rem(grp, 4) == g)
-            def _(g=g, kept=kept):
-                for at, row in enumerate(owned(g)):
-                    if row in kept:
-                        i = kept.index(row)
-                        self.red[at : at + 1, :] = total[i : i + 1, :]
+        red_ref[...] = total
 
     def drain(self):
-        for copy in self.a1 + self.a2 + self.b1 + self.b2:
-            copy.wait_send()
         for i in range(8):
             copy, away = self.last(i)
             pl.when(away)(copy.wait_send)
@@ -277,20 +275,17 @@
         pltpu.VMEM((NY, NX, half, 128), BF16),
         pltpu.VMEM((NY, NX, half, 128), BF16),
         pltpu.VMEM((NY, NX, half, 128), BF16),
-        pltpu.VMEM((NY - 1, NX, na, 128), BF16),
-        pltpu.VMEM((NX, na, 128), BF16),
-        pltpu.VMEM((NX - 1, na, 128), BF16),
+        pltpu.VMEM((NY - 1, NX, max(na, 16), 128), BF16),
+        pltpu.VMEM((NX, max(na, 16), 128), BF16),
+        pltpu.VMEM((NX - 1, max(na, 16), 128), BF16),
         pltpu.VMEM((NX - 1, NY, nb, 128), BF16),
         pltpu.VMEM((NY, nb, 128), BF16),
         pltpu.VMEM((NY - 1, nb, 128), BF16),
-        pltpu.VMEM((8, 8, 128), F32),
-        pltpu.VMEM((NZ, 8, 128), F32),
         dma((1,)), dma((1,)),
         dma((NY - 1,)), dma((NY - 1,)),
         dma((NX - 1,)), dma((NX - 1,)),
         dma((NX - 1,)), dma((NX - 1,)),
         dma((NY - 1,)), dma((NY - 1,)),
-        dma((8,)), dma((NZ,)),
     ]
 
 
@@ -301,7 +296,7 @@
     tok_ref, cot_ref, oce_ref, land_ref, wqkv_ref, wproj_ref, rb_ref,
     htok_ref, hcot_ref, hoce_ref, uu_ref, ug_ref, hu_ref, hg_ref,
     x_ref, c_ref, n_ref, inv_ref, mask_ref, h_ref, ht_ref, qkv_ref, dz_ref, do_ref, o_ref, dqkv_ref,
-    p_ref, bias_ref, db_ref, grad_ref, bt_ref, load_sem, store_sem, halo_s, halo_r, *rest,
+    p_ref, bias_ref, db_ref, grad_ref, bt_ref, f_ref, r3_ref, load_sem, store_sem, halo_s, halo_r, z_s, z_r, *rest,
 ):
     band = lax.axis_index("band")
     grp = lax.axis_index("grp")
@@ -480,29 +475,35 @@
     parts = []
     at = 0
     for rows, count, na in PARTS:
-        parts.append(Part(rows, count, na, rest[at : at + 24], here, send, (grad_ref, bt_ref), red_ref))
-        at += 24
-    first, second = parts
+        parts.append(Part(rows, count, na, rest[at : at + 20], here, send, (grad_ref, bt_ref)))
+        at += 20
+    first, second, third = parts
+    share = Share(f_ref, r3_ref, z_s, z_r, here)
 
     proj = dot_tn(o_ref[...], dz_ref[...])
     for k in range(3):
         grad_ref[9 + k] = proj[:, 128 * k : 128 * k + 128]
     backward(0)
     first.start()
+    for i in range(8):
+        f_ref[i, SLOTS:16, :] = jnp.zeros((16 - SLOTS, 128), F32)
     backward(1)
+    second.start()
     first.spread()
     backward(2)
     for i in range(6):
         bt_ref[128 * i : 128 * i + 128, 0:64] = db_ref[:, 128 * i : 128 * i + 128].T
-    second.start()
+    third.start()
+    second.spread()
     first.turn()
 
     wide_mask = jnp.concatenate([mask_ref[...]] * 3, 1)
     x_ref[...] = wide_mask * dot_nn(o_ref[...], wproj_ref[...])
+    third.spread()
     for i in range(4):
         uu_ref[i] = grid_row(x_ref, 1, i).astype(BF16)
-    second.spread()
     halo_u = send(uu_ref, hu_ref, halo_s.at[3], halo_r.at[3], after_id)
+    second.turn()
     c_ref[...] = dot_nt(dqkv_ref[...], wqkv_ref[...])
 
     def back(i, carry):
@@ -518,8 +519,8 @@
     for i in range(4):
         ug_ref[i] = grid_row(c_ref, 1, i).astype(BF16)
     halo_g = send(ug_ref, hg_ref, halo_s.at[4], halo_r.at[4], after_id)
-    first.share()
-    second.turn()
+    third.turn()
+    first.collect(f_ref)
     for i in range(4):
         row = grid_row(x_ref, 0, i).astype(BF16).astype(F32)
         block_ref[4 + i] = (tok_ref[4 + i].astype(F32) + row).astype(BF16)
@@ -528,7 +529,9 @@
     upper, lower = pl.ds(4, 4), pl.ds(0, 4)
     keep(block_ref.at[upper], block_hbm.at[upper])
     keep(grad_out_ref.at[upper], grad_hbm.at[upper])
-    second.share()
+    second.collect(f_ref)
+    third.collect(f_ref)
+    share.start()
     inner = jnp.broadcast_to(linear, (4, 48, C)) > 0
     halo_u.wait_recv()
     low = jnp.where(inner, hu_ref[...].astype(F32), 0.0)
@@ -538,14 +541,13 @@
     low = jnp.where(inner, hg_ref[...].astype(F32), 0.0)
     grad_out_ref[0:4] = (cot_ref[0:4].astype(F32) + low).astype(BF16)
     keep(grad_out_ref.at[lower], grad_hbm.at[lower])
-    first.finish()
-    red_ref[13:16, :] = jnp.zeros((3, 128), F32)
-    second.finish()
+    for part in parts:
+        part.drain()
+    share.finish(red_ref)
     keep(red_ref, red_hbm)
+    share.drain()
     for copy in halos + [halo_u, halo_g]:
         copy.wait_send()
-    first.drain()
-    second.drain()
     for copy in kept:
         copy.wait()
 
@@ -626,7 +628,9 @@
         pltpu.VMEM((64, 768), F32),
         pltpu.VMEM((12, C, 128), F32),
         pltpu.VMEM((768, 128), F32),
-        dma((7,)), dma((5,)), dma((5,)), dma((5,)),
+        pltpu.VMEM((8, 16, 128), F32),
+        pltpu.VMEM((NZ, 16, 128), F32),
+        dma((7,)), dma((5,)), dma((5,)), dma((5,)), dma((8,)), dma((NZ,)),
     ]
     for rows, count, na in PARTS:
         scratch += part_scratch(count, na)

time: 54.4 us -> 55 us (1.011)
  Pallas kernels: 53.6 us -> 54.2 us
where the time goes in v4:
time: 55 us; the launch traced here: 54.8 us
  Pallas kernels  54.2 us (99%)
  between operations  0.64 us (1%)
    pallas_call x1, Pallas kernels, local(): pl.pallas_call(kernel, out_shape=[grid, grid, jax.ShapeDtypeStruct((16, 1...  51.7 us
    pallas_call x1, Pallas kernels, local(): pl.pallas_call(place_kernel, out_shape=[grid, grid] + [jax.ShapeDtypeStru...  2.46 us

profile of v4, /device:TPU:1, one launch (start us, length us, event | category | flops | bytes accessed | tf_op | source)
XLA Modules:
  0.0 54.8 jit_solution(9672552841161724111)
XLA Ops:
  0.6 51.7 %window_block.1 = (bf16[8,48,384]{2,1,0:T(8,128)(2,1)}, bf16[8,48,384]{2,1,0:T(8,128)(2,1)}, f32[16,128]{1,0:T(8,128)}) custom-call(bf16[8,48,384]{2,1,0:T(8,128)(2,1)} %tok_hbm.1, bf16[8,48,384]{2,1,0:T(8,128)(2,1)} %cot_hbm.1, s32[8,48]{1,0:T(8,128)} %oce_hbm.1, s32[1,6]{1,0:T(1,128)} %land_hbm.1, bf16[384,1152]{1,0:T(8,128)(2,1)} %wqkv_hbm.1, ...), custom_call_target="tpu_custom_call" | custom-call | flops 1500000000 | bytes 5000000 | tf_op jit(solution)/shard_map/window_block/pallas_call | solution.py:637
  52.3 2.5 %outputs.1 = (bf16[8,48,384]{2,1,0:T(8,128)(2,1)}, bf16[8,48,384]{2,1,0:T(8,128)(2,1)}, f32[864]{0:T(1024)}, f32[288]{0:T(512)}, f32[96]{0:T(128)}) custom-call(bf16[8,48,384]{2,1,0:T(8,128)(2,1)} %get-tuple-element.8.block_hbm, bf16[8,48,384]{2,1,0:T(8,128)(2,1)} %get-tuple-element.9.grad_hbm, f32[16,128]{1,0:T(8,128)} %get-tuple-element.10.red_hbm), custom_call_target="tpu_custom_call" | custom-call | flops 10000 | bytes 1200000 | tf_op jit(solution)/shard_map/outputs/pallas_call | solution.py:653

commit v5 on v4

--- a/solution.py
+++ b/solution.py
@@ -30,8 +30,7 @@
 BIAS_ROWS = [("bias", j, 0) for j in range(3)]
 PARTS = [
     (qkv_rows(0) + PROJ_ROWS[:7], 16, 16),
-    (qkv_rows(1)[:8], 8, 0),
-    (qkv_rows(1)[8:] + qkv_rows(2) + PROJ_ROWS[7:] + BIAS_ROWS, 16, 16),
+    (qkv_rows(1) + qkv_rows(2) + PROJ_ROWS[7:] + BIAS_ROWS, 24, 16),
 ]
 SLOTS = 13
 
@@ -296,7 +295,7 @@
     tok_ref, cot_ref, oce_ref, land_ref, wqkv_ref, wproj_ref, rb_ref,
     htok_ref, hcot_ref, hoce_ref, uu_ref, ug_ref, hu_ref, hg_ref,
     x_ref, c_ref, n_ref, inv_ref, mask_ref, h_ref, ht_ref, qkv_ref, dz_ref, do_ref, o_ref, dqkv_ref,
-    p_ref, bias_ref, db_ref, grad_ref, bt_ref, f_ref, r3_ref, load_sem, store_sem, halo_s, halo_r, z_s, z_r, *rest,
+    p_ref, bias_ref, db_ref, grad_ref, bt_ref, f_ref, r3_ref, load_sem, store_sem, halo_s, halo_r, z_s, z_r, near_sem, *rest,
 ):
     band = lax.axis_index("band")
     grp = lax.axis_index("grp")
@@ -319,12 +318,25 @@
         loads[-1].start()
 
     barrier = pltpu.get_barrier_semaphore()
-    peers = [after_id, before_id]
-    peers += [(band, lax.rem(grp + d, 16)) for d in range(1, 16)]
-    peers += [(lax.rem(y + d, NY) * NX + x, grp) for d in range(1, NY)]
-    peers += [(y * NX + lax.rem(x + d, NX), grp) for d in range(1, NX)]
+
+
+    def at_z(d):
+        return (band, lax.rem(z + NZ + d, NZ) * 2 + core)
+
+    def at_y(d):
+        return (lax.rem(y + NY + d, NY) * NX + x, grp)
+
+    def at_x(d):
+        return (y * NX + lax.rem(x + NX + d, NX), grp)
+
+    peers = [after_id, before_id, (band, z * 2 + 1 - core)]
+    peers += [at(d) for at in (at_z, at_y, at_x) for d in (1, -1)]
     for peer in peers:
         pl.semaphore_signal(barrier, inc=1, device_id=peer, device_id_type=MESH)
+
+    def tell(r, at, d):
+        for to in (at(d), at(-d)):
+            pl.semaphore_signal(near_sem.at[r], inc=1, device_id=to, device_id_type=MESH)
 
     def send(src, dst, s, r, to):
         copy = pltpu.make_async_remote_copy(
@@ -343,6 +355,10 @@
     stage_rows([tok_ref[4 + i] for i in range(4)], 0, x_ref)
 
     pl.semaphore_wait(barrier, len(peers))
+    tell(0, at_z, 1)
+    tell(1, at_y, 1)
+    tell(2, at_x, 1)
+    far = (2, 3, 4)
     halos = [
         send(tok_hbm.at[pl.ds(0, 4)], htok_ref, halo_s.at[0], halo_r.at[0], before_id),
         send(oce_hbm, hoce_ref, halo_s.at[1], halo_r.at[1], before_id),
@@ -392,6 +408,10 @@
     stage_rows([jnp.where(here_lower, htok_ref[i].astype(F32), 0.0) for i in range(4)], 1, x_ref)
     lax.fori_loop(3, 6, norm, 0, unroll=3)
     project(1)
+    for r in (0, 1):
+        pl.semaphore_wait(near_sem.at[r], 2)
+    tell(3, at_z, 2)
+    tell(4, at_y, 2)
     ht_ref[...] = h_ref[...].T
     halos[1].wait_recv()
     ocean = jnp.where(jnp.broadcast_to(linear, (4, 48)) < 511, hoce_ref[0:4, :].astype(F32), 0.0)
@@ -477,7 +497,7 @@
     for rows, count, na in PARTS:
         parts.append(Part(rows, count, na, rest[at : at + 20], here, send, (grad_ref, bt_ref)))
         at += 20
-    first, second, third = parts
+    first, second = parts
     share = Share(f_ref, r3_ref, z_s, z_r, here)
 
     proj = dot_tn(o_ref[...], dz_ref[...])
@@ -488,22 +508,21 @@
     for i in range(8):
         f_ref[i, SLOTS:16, :] = jnp.zeros((16 - SLOTS, 128), F32)
     backward(1)
-    second.start()
+    for r in far:
+        pl.semaphore_wait(near_sem.at[r], 2)
     first.spread()
     backward(2)
     for i in range(6):
         bt_ref[128 * i : 128 * i + 128, 0:64] = db_ref[:, 128 * i : 128 * i + 128].T
-    third.start()
-    second.spread()
+    second.start()
     first.turn()
 
     wide_mask = jnp.concatenate([mask_ref[...]] * 3, 1)
     x_ref[...] = wide_mask * dot_nn(o_ref[...], wproj_ref[...])
-    third.spread()
+    second.spread()
     for i in range(4):
         uu_ref[i] = grid_row(x_ref, 1, i).astype(BF16)
     halo_u = send(uu_ref, hu_ref, halo_s.at[3], halo_r.at[3], after_id)
-    second.turn()
     c_ref[...] = dot_nt(dqkv_ref[...], wqkv_ref[...])
 
     def back(i, carry):
@@ -519,7 +538,7 @@
     for i in range(4):
         ug_ref[i] = grid_row(c_ref, 1, i).astype(BF16)
     halo_g = send(ug_ref, hg_ref, halo_s.at[4], halo_r.at[4], after_id)
-    third.turn()
+    second.turn()
     first.collect(f_ref)
     for i in range(4):
         row = grid_row(x_ref, 0, i).astype(BF16).astype(F32)
@@ -530,7 +549,6 @@
     keep(block_ref.at[upper], block_hbm.at[upper])
     keep(grad_out_ref.at[upper], grad_hbm.at[upper])
     second.collect(f_ref)
-    third.collect(f_ref)
     share.start()
     inner = jnp.broadcast_to(linear, (4, 48, C)) > 0
     halo_u.wait_recv()
@@ -631,6 +649,7 @@
         pltpu.VMEM((8, 16, 128), F32),
         pltpu.VMEM((NZ, 16, 128), F32),
         dma((7,)), dma((5,)), dma((5,)), dma((5,)), dma((8,)), dma((NZ,)),
+        pltpu.SemaphoreType.REGULAR((5,)),
     ]
     for rows, count, na in PARTS:
         scratch += part_scratch(count, na)

time: 55 us -> 53.3 us (0.969)
  Pallas kernels: 54.2 us -> 52.5 us
    pallas_call x1, Pallas kernels: 51.7 us -> 50 us  [local(): pl.pallas_call(kernel, out_shape=[grid, grid, jax.ShapeDtypeStruct((16, 1...]
where the time goes in v5:
time: 53.3 us; the launch traced here: 53.1 us
  Pallas kernels  52.5 us (98%)
  between operations  0.64 us (1%)
    pallas_call x1, Pallas kernels, local(): pl.pallas_call(kernel, out_shape=[grid, grid, jax.ShapeDtypeStruct((16, 1...  50 us
    pallas_call x1, Pallas kernels, local(): pl.pallas_call(place_kernel, out_shape=[grid, grid] + [jax.ShapeDtypeStru...  2.46 us

profile of v5, /device:TPU:1, one launch (start us, length us, event | category | flops | bytes accessed | tf_op | source)
XLA Modules:
  0.0 53.1 jit_solution(324764591853235486)
XLA Ops:
  0.6 50.0 %window_block.1 = (bf16[8,48,384]{2,1,0:T(8,128)(2,1)}, bf16[8,48,384]{2,1,0:T(8,128)(2,1)}, f32[16,128]{1,0:T(8,128)}) custom-call(bf16[8,48,384]{2,1,0:T(8,128)(2,1)} %tok_hbm.1, bf16[8,48,384]{2,1,0:T(8,128)(2,1)} %cot_hbm.1, s32[8,48]{1,0:T(8,128)} %oce_hbm.1, s32[1,6]{1,0:T(1,128)} %land_hbm.1, bf16[384,1152]{1,0:T(8,128)(2,1)} %wqkv_hbm.1, ...), custom_call_target="tpu_custom_call" | custom-call | flops 1500000000 | bytes 5000000 | tf_op jit(solution)/shard_map/window_block/pallas_call | solution.py:656
  50.7 2.5 %outputs.1 = (bf16[8,48,384]{2,1,0:T(8,128)(2,1)}, bf16[8,48,384]{2,1,0:T(8,128)(2,1)}, f32[864]{0:T(1024)}, f32[288]{0:T(512)}, f32[96]{0:T(128)}) custom-call(bf16[8,48,384]{2,1,0:T(8,128)(2,1)} %get-tuple-element.8.block_hbm, bf16[8,48,384]{2,1,0:T(8,128)(2,1)} %get-tuple-element.9.grad_hbm, f32[16,128]{1,0:T(8,128)} %get-tuple-element.10.red_hbm), custom_call_target="tpu_custom_call" | custom-call | flops 10000 | bytes 1200000 | tf_op jit(solution)/shard_map/outputs/pallas_call | solution.py:672

commit v6 on v5

--- a/solution.py
+++ b/solution.py
@@ -23,15 +23,14 @@
 
 
 def qkv_rows(g):
-    return [("qkv", j, k) for j in range(3) for k in (g, 3 + g, 6 + g)]
-
-
-PROJ_ROWS = [("proj", j, k) for j in range(3) for k in range(3)]
+    return [("qkv", j, k) for k in (g, 3 + g, 6 + g) for j in range(3)]
+
+
+PROJ_ROWS = [("proj", j, k) for k in range(3) for j in range(3)]
 BIAS_ROWS = [("bias", j, 0) for j in range(3)]
-PARTS = [
-    (qkv_rows(0) + PROJ_ROWS[:7], 16, 16),
-    (qkv_rows(1) + qkv_rows(2) + PROJ_ROWS[7:] + BIAS_ROWS, 24, 16),
-]
+GROUPS = [PROJ_ROWS + qkv_rows(0), qkv_rows(1), qkv_rows(2) + BIAS_ROWS]
+TURNS = [[0], [1, 2]]
+PADDED = 24
 SLOTS = 13
 
 
@@ -84,133 +83,100 @@
     return pltpu.roll(jnp.concatenate([src_ref[at : at + 8, :] for at in ats], 0), 4, 0)
 
 
-class Part:
-    def __init__(self, rows, count, along_y, refs, here, send, sources):
+class Group:
+    def __init__(self, rows, refs, here, send):
+        self.rows, self.n, self.here, self.send = rows, len(rows), here, send
         (
-            self.pk, self.pack, self.r0, self.s1, self.ra, self.ta, self.ra2, self.rb, self.tb, self.rb2,
-            self.core_s, self.core_r, self.a1_s, self.a1_r, self.a2_s, self.a2_r,
-            self.b1_s, self.b1_r, self.b2_s, self.b2_r,
+            self.pk, self.pack, self.r0, self.s1, self.rx,
+            self.core_s, self.core_r, self.x_s, self.x_r,
         ) = refs
-        self.rows, self.count, self.na = rows, count, along_y
-        self.half = 2 * count
-        self.nb = self.half - along_y
-        self.here, self.send, self.sources = here, send, sources
-        self.a1, self.a2, self.b1, self.b2 = [], [], [], []
 
     def start(self):
         band, grp, y, x, z, core = self.here
-        n = self.count
-        grad_ref, bt_ref = self.sources
-        lane = lax.broadcasted_iota(jnp.int32, (128, 128), 1)
-        for i, (kind, j, k) in enumerate(self.rows):
-            if kind == "bias":
-                even = bt_ref[pl.ds(2 * j, 128, stride=6), :]
-                odd = bt_ref[pl.ds(2 * j + 1, 128, stride=6), :]
-                value = jnp.where(lane < 64, even, pltpu.roll(odd, 64, 1))
-            else:
-                at = k if kind == "qkv" else 9 + k
-                value = grad_ref.at[at][pl.ds(j, 128, stride=3), :]
-            self.pk[pl.ds(i, 128, stride=n), :] = value
-        for i in range(len(self.rows), n):
-            self.pk[pl.ds(i, 128, stride=n), :] = jnp.zeros((128, 128), F32)
-        theirs = (1 - core) * self.half
+        theirs = pl.ds(pl.multiple_of((1 - core) * 64, 64), 64)
 
         def narrow(i, carry):
-            for j in range(NX):
-                at = pl.multiple_of((i * NX + j) * 4 * n + theirs, 16)
-                self.pack[i, j] = self.pk[pl.ds(at, self.half), :].astype(BF16)
+            self.pack[i] = self.pk[i, theirs, :].astype(BF16)
             return carry
 
-        lax.fori_loop(0, NY, narrow, 0)
+        lax.fori_loop(0, self.n, narrow, 0, unroll=3)
         self.core_copy = self.send(
             self.pack, self.r0, self.core_s.at[0], self.core_r.at[0], (band, z * 2 + 1 - core)
         )
 
     def spread(self):
         band, grp, y, x, z, core = self.here
-        n, na = self.count, self.na
-        mine = core * self.half
+        mine = pl.ds(pl.multiple_of(core * 64, 64), 64)
         self.core_copy.wait()
 
         def add(i, carry):
-            for j in range(NX):
-                at = pl.multiple_of((i * NX + j) * 4 * n + mine, 16)
-                total = self.pk[pl.ds(at, self.half), :] + self.r0[i, j].astype(F32)
-                self.s1[i, j] = total.astype(BF16)
+            self.s1[i] = (self.pk[i, mine, :] + self.r0[i].astype(F32)).astype(BF16)
             return carry
 
-        lax.fori_loop(0, NY, add, 0)
+        lax.fori_loop(0, self.n, add, 0, unroll=3)
+        self.sent = []
         for d in range(1, NX):
             to = lax.rem(x + d, NX)
-            self.b1.append(
+            self.sent.append(
                 self.send(
-                    self.s1.at[:, to, pl.ds(na, self.nb), :], self.rb.at[d - 1],
-                    self.b1_s.at[d - 1], self.b1_r.at[d - 1], (y * NX + to, grp),
+                    self.s1.at[:, pl.ds(pl.multiple_of(16 * to, 16), 16), :], self.rx.at[d - 1],
+                    self.x_s.at[d - 1], self.x_r.at[d - 1], (y * NX + to, grp),
                 )
             )
-        for d in range(1, NY if na else 1):
+
+    def turn(self, tb_ref, base):
+        band, grp, y, x, z, core = self.here
+        total = self.s1[:, pl.ds(pl.multiple_of(16 * x, 16), 16), :].astype(F32)
+        for d in range(1, NX):
+            self.sent[d - 1].wait_recv()
+            total = total + self.rx[d - 1].astype(F32)
+        for i in range(self.n):
+            for quarter in range(2):
+                at = pl.ds(quarter * PADDED + base + i, NY, stride=2 * PADDED)
+                tb_ref[at, :] = total[i, 8 * quarter : 8 * quarter + 8, :]
+
+
+class Turn:
+    def __init__(self, groups, refs, here, send):
+        self.groups, self.here, self.send = groups, here, send
+        self.rows = [row for group in groups for row in group.rows]
+        self.wide, self.tb, self.ry, self.y_s, self.y_r = refs
+
+    def clear(self):
+        for i in range(len(self.rows), PADDED):
+            for quarter in range(2):
+                at = pl.ds(quarter * PADDED + i, NY, stride=2 * PADDED)
+                self.wide[at, :] = jnp.zeros((NY, 128), F32)
+
+    def start(self):
+        band, grp, y, x, z, core = self.here
+        base = 0
+        for group in self.groups:
+            group.turn(self.wide, base)
+            base += group.n
+        for i in range(NY):
+            self.tb[i] = self.wide[2 * PADDED * i : 2 * PADDED * (i + 1), :].astype(BF16)
+        self.sent = []
+        for d in range(1, NY):
             to = lax.rem(y + d, NY)
-            self.a1.append(
+            self.sent.append(
                 self.send(
-                    self.s1.at[to, :, pl.ds(0, na), :], self.ra.at[d - 1],
-                    self.a1_s.at[d - 1], self.a1_r.at[d - 1], (to * NX + x, grp),
+                    self.tb.at[to], self.ry.at[d - 1],
+                    self.y_s.at[d - 1], self.y_r.at[d - 1], (to * NX + x, grp),
                 )
             )
 
-    def turn(self):
-        band, grp, y, x, z, core = self.here
-        na = self.na
-        total = self.s1[:, x, na : self.half, :].astype(F32)
-        for d in range(1, NX):
-            self.b1[d - 1].wait_recv()
-            total = total + self.rb[d - 1].astype(F32)
-        self.tb[...] = total.astype(BF16)
-        for d in range(1, NY):
-            to = lax.rem(y + d, NY)
-            self.b2.append(
-                self.send(
-                    self.tb.at[to], self.rb2.at[d - 1],
-                    self.b2_s.at[d - 1], self.b2_r.at[d - 1], (to * NX + x, grp),
-                )
-            )
-        if not na:
-            return
-        total = self.s1[y, :, 0:na, :].astype(F32)
-        for d in range(1, NY):
-            self.a1[d - 1].wait_recv()
-            total = total + self.ra[d - 1].astype(F32)
-        self.ta[...] = total.astype(BF16)
-        for d in range(1, NX):
-            to = lax.rem(x + d, NX)
-            self.a2.append(
-                self.send(
-                    self.ta.at[to], self.ra2.at[d - 1],
-                    self.a2_s.at[d - 1], self.a2_r.at[d - 1], (y * NX + to, grp),
-                )
-            )
-
     def collect(self, f_ref):
         band, grp, y, x, z, core = self.here
-        n, na = self.count, self.na
-        total = self.tb[y].astype(F32)
+        total = self.wide[pl.ds(pl.multiple_of(y * 2 * PADDED, 8), 2 * PADDED), :]
         for d in range(1, NY):
-            self.b2[d - 1].wait_recv()
-            total = total + self.rb2[d - 1].astype(F32)
-        if na:
-            low = self.ta[x].astype(F32)
-            for d in range(1, NX):
-                self.a2[d - 1].wait_recv()
-                low = low + self.ra2[d - 1].astype(F32)
-            total = jnp.concatenate([low, total], 0)
+            self.sent[d - 1].wait_recv()
+            total = total + self.ry[d - 1].astype(F32)
         for i in range(8):
             for at, row in enumerate(owned(i % 4)):
                 if row in self.rows:
-                    first = n * (i // 4) + self.rows.index(row)
+                    first = PADDED * (i // 4) + self.rows.index(row)
                     f_ref[i, at : at + 1, :] = total[first : first + 1, :]
-
-    def drain(self):
-        for copy in self.a1 + self.a2 + self.b1 + self.b2:
-            copy.wait_send()
 
 
 class Share:
@@ -265,27 +231,37 @@
             pl.when(away)(copy.wait_send)
 
 
-def part_scratch(count, na):
-    half = 2 * count
-    nb = half - na
+def group_scratch(n):
     dma = pltpu.SemaphoreType.DMA
     return [
-        pltpu.VMEM((128 * count, 128), F32),
-        pltpu.VMEM((NY, NX, half, 128), BF16),
-        pltpu.VMEM((NY, NX, half, 128), BF16),
-        pltpu.VMEM((NY, NX, half, 128), BF16),
-        pltpu.VMEM((NY - 1, NX, max(na, 16), 128), BF16),
-        pltpu.VMEM((NX, max(na, 16), 128), BF16),
-        pltpu.VMEM((NX - 1, max(na, 16), 128), BF16),
-        pltpu.VMEM((NX - 1, NY, nb, 128), BF16),
-        pltpu.VMEM((NY, nb, 128), BF16),
-        pltpu.VMEM((NY - 1, nb, 128), BF16),
-        dma((1,)), dma((1,)),
-        dma((NY - 1,)), dma((NY - 1,)),
-        dma((NX - 1,)), dma((NX - 1,)),
-        dma((NX - 1,)), dma((NX - 1,)),
+        pltpu.VMEM((n, 128, 128), F32),
+        pltpu.VMEM((n, 64, 128), BF16),
+        pltpu.VMEM((n, 64, 128), BF16),
+        pltpu.VMEM((n, 64, 128), BF16),
+        pltpu.VMEM((NX - 1, n, 16, 128), BF16),
+        dma((1,)), dma((1,)), dma((NX - 1,)), dma((NX - 1,)),
+    ]
+
+
+def turn_scratch():
+    dma = pltpu.SemaphoreType.DMA
+    return [
+        pltpu.VMEM((NY * 2 * PADDED, 128), F32),
+        pltpu.VMEM((NY, 2 * PADDED, 128), BF16),
+        pltpu.VMEM((NY - 1, 2 * PADDED, 128), BF16),
         dma((NY - 1,)), dma((NY - 1,)),
     ]
+
+
+def permutation():
+    at = lax.broadcasted_iota(jnp.int32, (C, C), 0)
+    feature = lax.broadcasted_iota(jnp.int32, (C, C), 1)
+
+    def bits(low, count):
+        return lax.bitwise_and(lax.shift_right_logical(at, jnp.full_like(at, low)), (1 << count) - 1)
+
+    m = 16 * bits(0, 3) + bits(3, 1) + 4 * bits(4, 2) + 2 * bits(6, 1)
+    return (feature == 3 * m + bits(7, 2)).astype(F32).astype(BF16)
 
 
 def kernel(
@@ -294,8 +270,8 @@
     block_ref, grad_out_ref, red_ref,
     tok_ref, cot_ref, oce_ref, land_ref, wqkv_ref, wproj_ref, rb_ref,
     htok_ref, hcot_ref, hoce_ref, uu_ref, ug_ref, hu_ref, hg_ref,
-    x_ref, c_ref, n_ref, inv_ref, mask_ref, h_ref, ht_ref, qkv_ref, dz_ref, do_ref, o_ref, dqkv_ref,
-    p_ref, bias_ref, db_ref, grad_ref, bt_ref, f_ref, r3_ref, load_sem, store_sem, halo_s, halo_r, z_s, z_r, near_sem, *rest,
+    x_ref, c_ref, n_ref, inv_ref, mask_ref, h_ref, ht_ref, qkv_ref, dz_ref, do_ref, o_ref, dqkv_ref, ot_ref,
+    p_ref, bias_ref, db_ref, perm_ref, bt_ref, f_ref, r3_ref, load_sem, store_sem, halo_s, halo_r, z_s, z_r, near_sem, *rest,
 ):
     band = lax.axis_index("band")
     grp = lax.axis_index("grp")
@@ -307,12 +283,14 @@
     after_id = (after // 16, lax.rem(after, 16))
     before_id = (before // 16, lax.rem(before, 16))
 
+    def blocks(ref, i, j):
+        return ref.at[:, pl.ds(C * i + 128 * j, 128)]
+
     loads = []
     for i, (src, dst) in enumerate(
-        (
-            (tok_hbm, tok_ref), (oce_hbm, oce_ref), (land_hbm, land_ref), (wqkv_hbm, wqkv_ref),
-            (cot_hbm, cot_ref), (wproj_hbm, wproj_ref), (rb_hbm, rb_ref),
-        )
+        [(tok_hbm, tok_ref), (oce_hbm, oce_ref), (land_hbm, land_ref), (cot_hbm, cot_ref)]
+        + [(wproj_hbm, wproj_ref), (rb_hbm, rb_ref)]
+        + [(blocks(wqkv_hbm, i, j), blocks(wqkv_ref, j, i)) for j in range(HG) for i in range(3)]
     ):
         loads.append(pltpu.make_async_copy(src, dst, load_sem.at[i]))
         loads[-1].start()
@@ -353,6 +331,7 @@
 
     loads[0].wait()
     stage_rows([tok_ref[4 + i] for i in range(4)], 0, x_ref)
+    perm_ref[...] = permutation()
 
     pl.semaphore_wait(barrier, len(peers))
     tell(0, at_z, 1)
@@ -391,13 +370,14 @@
     loads[2].wait()
     land = land_ref[...].astype(F32)
     stage_mask(oce_ref[4:8, :].astype(F32), land, 0, mask_ref)
+    for i in range(6, 15):
+        loads[i].wait()
+    project(0)
     loads[3].wait()
-    project(0)
+    stage_rows([cot_ref[4 + i] for i in range(4)], 0, c_ref)
     loads[4].wait()
-    stage_rows([cot_ref[4 + i] for i in range(4)], 0, c_ref)
+    pull(0)
     loads[5].wait()
-    pull(0)
-    loads[6].wait()
     for i in range(6):
         pair = jnp.concatenate([rb_ref[2 * i], rb_ref[2 * i + 1]], 0)
         bias_ref[:, 128 * i : 128 * i + 128] = pair.T
@@ -412,7 +392,7 @@
         pl.semaphore_wait(near_sem.at[r], 2)
     tell(3, at_z, 2)
     tell(4, at_y, 2)
-    ht_ref[...] = h_ref[...].T
+    ht_ref[...] = dot_nt(perm_ref[...], h_ref[...]).astype(BF16)
     halos[1].wait_recv()
     ocean = jnp.where(jnp.broadcast_to(linear, (4, 48)) < 511, hoce_ref[0:4, :].astype(F32), 0.0)
     stage_mask(ocean, land, 1, mask_ref)
@@ -445,7 +425,7 @@
         ref[second, lanes] = value[32:64]
 
     def lanes_of(g):
-        return [slice(C * i + 128 * g, C * i + 128 * g + 128) for i in range(3)] + [
+        return [slice(C * g + 128 * i, C * g + 128 * i + 128) for i in range(3)] + [
             slice(256 * g, 256 * g + 256)
         ]
 
@@ -460,7 +440,7 @@
             weights = jnp.exp(s - jnp.max(s, 0, keepdims=True))
             p = weights * (1.0 / jnp.sum(weights, 0, keepdims=True))
             p_ref[whole, wide] = p
-            store(o_ref, w, q_lanes, fold(dot_tn(p.astype(BF16), load(qkv_ref, w, v_lanes))).astype(BF16))
+            store(o_ref, w, slice(128 * g, 128 * g + 128), fold(dot_tn(p.astype(BF16), load(qkv_ref, w, v_lanes))).astype(BF16))
         return carry
 
     def backward(g):
@@ -469,7 +449,7 @@
         def step(w, carry):
             whole = pl.ds(pl.multiple_of(w * 64, 64), 64)
             q4 = spread(load(qkv_ref, w, q_lanes))
-            do4 = spread(load(do_ref, w, q_lanes))
+            do4 = spread(load(do_ref, w, slice(128 * g, 128 * g + 128)))
             p = p_ref[whole, wide]
             dp = dot_nt(load(qkv_ref, w, v_lanes), do4)
             store(dqkv_ref, w, v_lanes, dot_nn(p.astype(BF16), do4).astype(BF16))
@@ -482,8 +462,7 @@
             return carry
 
         lax.fori_loop(0, WB, step, 0, unroll=6)
-        for k in (g, 3 + g, 6 + g):
-            grad_ref[k] = dot_nn(ht_ref[...], dqkv_ref[:, 128 * k : 128 * k + 128])
+        fill(groups[g], dot_nn(ht_ref[...], dqkv_ref[:, C * g : C * g + C]), 9 if g == 0 else 0)
 
     lax.fori_loop(0, WB, forward, 0, unroll=2)
 
@@ -492,37 +471,53 @@
     pull(1)
 
     here = (band, grp, y, x, z, core)
-    parts = []
+    groups, turns = [], []
     at = 0
-    for rows, count, na in PARTS:
-        parts.append(Part(rows, count, na, rest[at : at + 20], here, send, (grad_ref, bt_ref)))
-        at += 20
-    first, second = parts
+    for rows in GROUPS:
+        groups.append(Group(rows, rest[at : at + 9], here, send))
+        at += 9
+    for members in TURNS:
+        turns.append(Turn([groups[i] for i in members], rest[at : at + 5], here, send))
+        at += 5
     share = Share(f_ref, r3_ref, z_s, z_r, here)
 
-    proj = dot_tn(o_ref[...], dz_ref[...])
-    for k in range(3):
-        grad_ref[9 + k] = proj[:, 128 * k : 128 * k + 128]
+    def fill(group, value, base):
+        for k in range(3):
+            for j in range(3):
+                group.pk[base + 3 * k + j] = value[128 * j : 128 * j + 128, 128 * k : 128 * k + 128]
+
+    ot_ref[...] = dot_nt(perm_ref[...], o_ref[...]).astype(BF16)
+    fill(groups[0], dot_nn(ot_ref[...], dz_ref[...]), 0)
     backward(0)
-    first.start()
+    groups[0].start()
     for i in range(8):
         f_ref[i, SLOTS:16, :] = jnp.zeros((16 - SLOTS, 128), F32)
+    for turn in turns:
+        turn.clear()
     backward(1)
+    groups[1].start()
     for r in far:
         pl.semaphore_wait(near_sem.at[r], 2)
-    first.spread()
+    groups[0].spread()
     backward(2)
     for i in range(6):
         bt_ref[128 * i : 128 * i + 128, 0:64] = db_ref[:, 128 * i : 128 * i + 128].T
-    second.start()
-    first.turn()
+    lane = lax.broadcasted_iota(jnp.int32, (8, 128), 1)
+    for j in range(3):
+        for i in range(16):
+            first = 2 * j + 24 * ((i // 2) % 4) + 12 * (i // 8) + 6 * (i % 2)
+            even = bt_ref[pl.ds(first, 8, stride=96), :]
+            odd = bt_ref[pl.ds(first + 1, 8, stride=96), :]
+            groups[2].pk[9 + j, 8 * i : 8 * i + 8, :] = jnp.where(lane < 64, even, pltpu.roll(odd, 64, 1))
+    groups[2].start()
+    groups[1].spread()
 
     wide_mask = jnp.concatenate([mask_ref[...]] * 3, 1)
     x_ref[...] = wide_mask * dot_nn(o_ref[...], wproj_ref[...])
-    second.spread()
+    groups[2].spread()
+    turns[0].start()
     for i in range(4):
         uu_ref[i] = grid_row(x_ref, 1, i).astype(BF16)
-    halo_u = send(uu_ref, hu_ref, halo_s.at[3], halo_r.at[3], after_id)
     c_ref[...] = dot_nt(dqkv_ref[...], wqkv_ref[...])
 
     def back(i, carry):
@@ -537,9 +532,10 @@
     lax.fori_loop(0, WB, back, 0, unroll=3)
     for i in range(4):
         ug_ref[i] = grid_row(c_ref, 1, i).astype(BF16)
+    turns[1].start()
+    halo_u = send(uu_ref, hu_ref, halo_s.at[3], halo_r.at[3], after_id)
     halo_g = send(ug_ref, hg_ref, halo_s.at[4], halo_r.at[4], after_id)
-    second.turn()
-    first.collect(f_ref)
+    turns[0].collect(f_ref)
     for i in range(4):
         row = grid_row(x_ref, 0, i).astype(BF16).astype(F32)
         block_ref[4 + i] = (tok_ref[4 + i].astype(F32) + row).astype(BF16)
@@ -548,7 +544,7 @@
     upper, lower = pl.ds(4, 4), pl.ds(0, 4)
     keep(block_ref.at[upper], block_hbm.at[upper])
     keep(grad_out_ref.at[upper], grad_hbm.at[upper])
-    second.collect(f_ref)
+    turns[1].collect(f_ref)
     share.start()
     inner = jnp.broadcast_to(linear, (4, 48, C)) > 0
     halo_u.wait_recv()
@@ -559,8 +555,9 @@
     low = jnp.where(inner, hg_ref[...].astype(F32), 0.0)
     grad_out_ref[0:4] = (cot_ref[0:4].astype(F32) + low).astype(BF16)
     keep(grad_out_ref.at[lower], grad_hbm.at[lower])
-    for part in parts:
-        part.drain()
+    for one in groups + turns:
+        for copy in one.sent:
+            copy.wait_send()
     share.finish(red_ref)
     keep(red_ref, red_hbm)
     share.drain()
@@ -641,18 +638,21 @@
         pltpu.VMEM((C, C), BF16),
         pltpu.VMEM((C, C), BF16),
         pltpu.VMEM((C, 3 * C), BF16),
+        pltpu.VMEM((C, C), BF16),
         pltpu.VMEM((C, 768), F32),
         pltpu.VMEM((64, 768), F32),
         pltpu.VMEM((64, 768), F32),
-        pltpu.VMEM((12, C, 128), F32),
+        pltpu.VMEM((C, C), BF16),
         pltpu.VMEM((768, 128), F32),
         pltpu.VMEM((8, 16, 128), F32),
         pltpu.VMEM((NZ, 16, 128), F32),
-        dma((7,)), dma((5,)), dma((5,)), dma((5,)), dma((8,)), dma((NZ,)),
+        dma((15,)), dma((5,)), dma((5,)), dma((5,)), dma((8,)), dma((NZ,)),
         pltpu.SemaphoreType.REGULAR((5,)),
     ]
-    for rows, count, na in PARTS:
-        scratch += part_scratch(count, na)
+    for rows in GROUPS:
+        scratch += group_scratch(len(rows))
+    for members in TURNS:
+        scratch += turn_scratch()
     block_out, token_grad, red = pl.pallas_call(
         kernel,
         out_shape=[grid, grid, jax.ShapeDtypeStruct((16, 128), F32)],

time: 53.3 us -> 53 us (level)
  no operation moved by 1% of the time
where the time goes in v6:
time: 53 us; the launch traced here: 52.8 us
  Pallas kernels  52.2 us (98%)
  between operations  0.64 us (1%)
    pallas_call x1, Pallas kernels, local(): pl.pallas_call(kernel, out_shape=[grid, grid, jax.ShapeDtypeStruct((16, 1...  49.7 us
    pallas_call x1, Pallas kernels, local(): pl.pallas_call(place_kernel, out_shape=[grid, grid] + [jax.ShapeDtypeStru...  2.46 us

profile of v6, /device:TPU:1, one launch (start us, length us, event | category | flops | bytes accessed | tf_op | source)
XLA Modules:
  0.0 52.8 jit_solution(7910812387486637930)
XLA Ops:
  0.6 49.7 %window_block.1 = (bf16[8,48,384]{2,1,0:T(8,128)(2,1)}, bf16[8,48,384]{2,1,0:T(8,128)(2,1)}, f32[16,128]{1,0:T(8,128)}) custom-call(bf16[8,48,384]{2,1,0:T(8,128)(2,1)} %tok_hbm.1, bf16[8,48,384]{2,1,0:T(8,128)(2,1)} %cot_hbm.1, s32[8,48]{1,0:T(8,128)} %oce_hbm.1, s32[1,6]{1,0:T(1,128)} %land_hbm.1, bf16[384,1152]{1,0:T(8,128)(2,1)} %wqkv_hbm.1, ...), custom_call_target="tpu_custom_call" | custom-call | flops 1500000000 | bytes 5000000 | tf_op jit(solution)/shard_map/window_block/pallas_call | solution.py:656
  50.4 2.5 %outputs.1 = (bf16[8,48,384]{2,1,0:T(8,128)(2,1)}, bf16[8,48,384]{2,1,0:T(8,128)(2,1)}, f32[864]{0:T(1024)}, f32[288]{0:T(512)}, f32[96]{0:T(128)}) custom-call(bf16[8,48,384]{2,1,0:T(8,128)(2,1)} %get-tuple-element.8.block_hbm, bf16[8,48,384]{2,1,0:T(8,128)(2,1)} %get-tuple-element.9.grad_hbm, f32[16,128]{1,0:T(8,128)} %get-tuple-element.10.red_hbm), custom_call_target="tpu_custom_call" | custom-call | flops 10000 | bytes 1200000 | tf_op jit(solution)/shard_map/outputs/pallas_call | solution.py:672

commit v7 on v6

--- a/solution.py
+++ b/solution.py
@@ -28,9 +28,7 @@
 
 PROJ_ROWS = [("proj", j, k) for k in range(3) for j in range(3)]
 BIAS_ROWS = [("bias", j, 0) for j in range(3)]
-GROUPS = [PROJ_ROWS + qkv_rows(0), qkv_rows(1), qkv_rows(2) + BIAS_ROWS]
-TURNS = [[0], [1, 2]]
-PADDED = 24
+GROUPS = [PROJ_ROWS + qkv_rows(0), qkv_rows(1)[:8], qkv_rows(1)[8:] + qkv_rows(2) + BIAS_ROWS]
 SLOTS = 13
 
 
@@ -124,7 +122,7 @@
                 )
             )
 
-    def turn(self, tb_ref, base):
+    def take(self, wide_ref, padded):
         band, grp, y, x, z, core = self.here
         total = self.s1[:, pl.ds(pl.multiple_of(16 * x, 16), 16), :].astype(F32)
         for d in range(1, NX):
@@ -132,30 +130,32 @@
             total = total + self.rx[d - 1].astype(F32)
         for i in range(self.n):
             for quarter in range(2):
-                at = pl.ds(quarter * PADDED + base + i, NY, stride=2 * PADDED)
-                tb_ref[at, :] = total[i, 8 * quarter : 8 * quarter + 8, :]
+                at = pl.ds(quarter * padded + i, NY, stride=2 * padded)
+                wide_ref[at, :] = total[i, 8 * quarter : 8 * quarter + 8, :]
+
+
+def padded_of(n):
+    return -(-n // 8) * 8
 
 
 class Turn:
-    def __init__(self, groups, refs, here, send):
-        self.groups, self.here, self.send = groups, here, send
-        self.rows = [row for group in groups for row in group.rows]
+    def __init__(self, group, refs, here, send):
+        self.group, self.here, self.send = group, here, send
+        self.rows, self.padded = group.rows, padded_of(group.n)
         self.wide, self.tb, self.ry, self.y_s, self.y_r = refs
 
     def clear(self):
-        for i in range(len(self.rows), PADDED):
+        for i in range(len(self.rows), self.padded):
             for quarter in range(2):
-                at = pl.ds(quarter * PADDED + i, NY, stride=2 * PADDED)
+                at = pl.ds(quarter * self.padded + i, NY, stride=2 * self.padded)
                 self.wide[at, :] = jnp.zeros((NY, 128), F32)
 
     def start(self):
         band, grp, y, x, z, core = self.here
-        base = 0
-        for group in self.groups:
-            group.turn(self.wide, base)
-            base += group.n
+        n = 2 * self.padded
+        self.group.take(self.wide, self.padded)
         for i in range(NY):
-            self.tb[i] = self.wide[2 * PADDED * i : 2 * PADDED * (i + 1), :].astype(BF16)
+            self.tb[i] = self.wide[n * i : n * (i + 1), :].astype(BF16)
         self.sent = []
         for d in range(1, NY):
             to = lax.rem(y + d, NY)
@@ -168,20 +168,21 @@
 
     def collect(self, f_ref):
         band, grp, y, x, z, core = self.here
-        total = self.wide[pl.ds(pl.multiple_of(y * 2 * PADDED, 8), 2 * PADDED), :]
+        n = 2 * self.padded
+        total = self.wide[pl.ds(pl.multiple_of(y * n, 8), n), :]
         for d in range(1, NY):
             self.sent[d - 1].wait_recv()
             total = total + self.ry[d - 1].astype(F32)
         for i in range(8):
             for at, row in enumerate(owned(i % 4)):
                 if row in self.rows:
-                    first = PADDED * (i // 4) + self.rows.index(row)
+                    first = self.padded * (i // 4) + self.rows.index(row)
                     f_ref[i, at : at + 1, :] = total[first : first + 1, :]
 
 
 class Share:
-    def __init__(self, f_ref, r3_ref, z_s, z_r, here):
-        self.f, self.r3, self.z_s, self.z_r, self.here = f_ref, r3_ref, z_s, z_r, here
+    def __init__(self, wide_ref, f_ref, r3_ref, z_s, z_r, here):
+        self.wide, self.f, self.r3, self.z_s, self.z_r, self.here = wide_ref, f_ref, r3_ref, z_s, z_r, here
 
     def last(self, i):
         band, grp, y, x, z, core = self.here
@@ -198,6 +199,7 @@
         return copy, jnp.logical_or(to_z != z, core != to_core)
 
     def start(self):
+        self.f[...] = self.wide[...].astype(BF16)
         for i in range(8):
             copy, away = self.last(i)
             pl.when(away)(copy.start)
@@ -220,9 +222,9 @@
                 device_id_type=MESH,
             )
             pl.when(jnp.logical_or(z != s, core != own_core))(come.wait_recv)
-        total = self.r3[0]
+        total = self.r3[0].astype(F32)
         for s in range(1, NZ):
-            total = total + self.r3[s]
+            total = total + self.r3[s].astype(F32)
         red_ref[...] = total
 
     def drain(self):
@@ -243,12 +245,13 @@
     ]
 
 
-def turn_scratch():
+def turn_scratch(n):
     dma = pltpu.SemaphoreType.DMA
+    wide = 2 * padded_of(n)
     return [
-        pltpu.VMEM((NY * 2 * PADDED, 128), F32),
-        pltpu.VMEM((NY, 2 * PADDED, 128), BF16),
-        pltpu.VMEM((NY - 1, 2 * PADDED, 128), BF16),
+        pltpu.VMEM((NY * wide, 128), F32),
+        pltpu.VMEM((NY, wide, 128), BF16),
+        pltpu.VMEM((NY - 1, wide, 128), BF16),
         dma((NY - 1,)), dma((NY - 1,)),
     ]
 
@@ -271,7 +274,7 @@
     tok_ref, cot_ref, oce_ref, land_ref, wqkv_ref, wproj_ref, rb_ref,
     htok_ref, hcot_ref, hoce_ref, uu_ref, ug_ref, hu_ref, hg_ref,
     x_ref, c_ref, n_ref, inv_ref, mask_ref, h_ref, ht_ref, qkv_ref, dz_ref, do_ref, o_ref, dqkv_ref, ot_ref,
-    p_ref, bias_ref, db_ref, perm_ref, bt_ref, f_ref, r3_ref, load_sem, store_sem, halo_s, halo_r, z_s, z_r, near_sem, *rest,
+    p_ref, bias_ref, db_ref, perm_ref, bt_ref, f_ref, low_ref, r3_ref, load_sem, store_sem, halo_s, halo_r, z_s, z_r, near_sem, *rest,
 ):
     band = lax.axis_index("band")
     grp = lax.axis_index("grp")
@@ -283,6 +286,23 @@
     after_id = (after // 16, lax.rem(after, 16))
     before_id = (before // 16, lax.rem(before, 16))
 
+    barrier = pltpu.get_barrier_semaphore()
+
+
+    def at_z(d):
+        return (band, lax.rem(z + NZ + d, NZ) * 2 + core)
+
+    def at_y(d):
+        return (lax.rem(y + NY + d, NY) * NX + x, grp)
+
+    def at_x(d):
+        return (y * NX + lax.rem(x + NX + d, NX), grp)
+
+    peers = [after_id, before_id, (band, z * 2 + 1 - core)]
+    peers += [at(d) for at in (at_z, at_y, at_x) for d in (1, -1)]
+    for peer in peers:
+        pl.semaphore_signal(barrier, inc=1, device_id=peer, device_id_type=MESH)
+
     def blocks(ref, i, j):
         return ref.at[:, pl.ds(C * i + 128 * j, 128)]
 
@@ -295,23 +315,6 @@
         loads.append(pltpu.make_async_copy(src, dst, load_sem.at[i]))
         loads[-1].start()
 
-    barrier = pltpu.get_barrier_semaphore()
-
-
-    def at_z(d):
-        return (band, lax.rem(z + NZ + d, NZ) * 2 + core)
-
-    def at_y(d):
-        return (lax.rem(y + NY + d, NY) * NX + x, grp)
-
-    def at_x(d):
-        return (y * NX + lax.rem(x + NX + d, NX), grp)
-
-    peers = [after_id, before_id, (band, z * 2 + 1 - core)]
-    peers += [at(d) for at in (at_z, at_y, at_x) for d in (1, -1)]
-    for peer in peers:
-        pl.semaphore_signal(barrier, inc=1, device_id=peer, device_id_type=MESH)
-
     def tell(r, at, d):
         for to in (at(d), at(-d)):
             pl.semaphore_signal(near_sem.at[r], inc=1, device_id=to, device_id_type=MESH)
@@ -328,10 +331,6 @@
     def keep(src, dst):
         kept.append(pltpu.make_async_copy(src, dst, store_sem.at[len(kept)]))
         kept[-1].start()
-
-    loads[0].wait()
-    stage_rows([tok_ref[4 + i] for i in range(4)], 0, x_ref)
-    perm_ref[...] = permutation()
 
     pl.semaphore_wait(barrier, len(peers))
     tell(0, at_z, 1)
@@ -343,6 +342,10 @@
         send(oce_hbm, hoce_ref, halo_s.at[1], halo_r.at[1], before_id),
         send(cot_hbm.at[pl.ds(0, 4)], hcot_ref, halo_s.at[2], halo_r.at[2], before_id),
     ]
+
+    loads[0].wait()
+    stage_rows([tok_ref[4 + i] for i in range(4)], 0, x_ref)
+    perm_ref[...] = permutation()
 
     def norm(i, carry):
         rows = pl.ds(pl.multiple_of(i * 64, 64), 64)
@@ -462,7 +465,7 @@
             return carry
 
         lax.fori_loop(0, WB, step, 0, unroll=6)
-        fill(groups[g], dot_nn(ht_ref[...], dqkv_ref[:, C * g : C * g + C]), 9 if g == 0 else 0)
+        fill(qkv_rows(g), dot_nn(ht_ref[...], dqkv_ref[:, C * g : C * g + C]))
 
     lax.fori_loop(0, WB, forward, 0, unroll=2)
 
@@ -476,18 +479,21 @@
     for rows in GROUPS:
         groups.append(Group(rows, rest[at : at + 9], here, send))
         at += 9
-    for members in TURNS:
-        turns.append(Turn([groups[i] for i in members], rest[at : at + 5], here, send))
+    for group in groups:
+        turns.append(Turn(group, rest[at : at + 5], here, send))
         at += 5
-    share = Share(f_ref, r3_ref, z_s, z_r, here)
-
-    def fill(group, value, base):
-        for k in range(3):
-            for j in range(3):
-                group.pk[base + 3 * k + j] = value[128 * j : 128 * j + 128, 128 * k : 128 * k + 128]
+    share = Share(f_ref, low_ref, r3_ref, z_s, z_r, here)
+
+    def fill(rows, value):
+        for i, row in enumerate(rows):
+            j, k = i % 3, i // 3
+            for group in groups:
+                if row in group.rows:
+                    at = group.rows.index(row)
+                    group.pk[at] = value[128 * j : 128 * j + 128, 128 * k : 128 * k + 128]
 
     ot_ref[...] = dot_nt(perm_ref[...], o_ref[...]).astype(BF16)
-    fill(groups[0], dot_nn(ot_ref[...], dz_ref[...]), 0)
+    fill(PROJ_ROWS, dot_nn(ot_ref[...], dz_ref[...]))
     backward(0)
     groups[0].start()
     for i in range(8):
@@ -508,7 +514,7 @@
             first = 2 * j + 24 * ((i // 2) % 4) + 12 * (i // 8) + 6 * (i % 2)
             even = bt_ref[pl.ds(first, 8, stride=96), :]
             odd = bt_ref[pl.ds(first + 1, 8, stride=96), :]
-            groups[2].pk[9 + j, 8 * i : 8 * i + 8, :] = jnp.where(lane < 64, even, pltpu.roll(odd, 64, 1))
+            groups[2].pk[groups[2].n - 3 + j, 8 * i : 8 * i + 8, :] = jnp.where(lane < 64, even, pltpu.roll(odd, 64, 1))
     groups[2].start()
     groups[1].spread()
 
@@ -533,6 +539,7 @@
     for i in range(4):
         ug_ref[i] = grid_row(c_ref, 1, i).astype(BF16)
     turns[1].start()
+    turns[2].start()
     halo_u = send(uu_ref, hu_ref, halo_s.at[3], halo_r.at[3], after_id)
     halo_g = send(ug_ref, hg_ref, halo_s.at[4], halo_r.at[4], after_id)
     turns[0].collect(f_ref)
@@ -545,6 +552,7 @@
     keep(block_ref.at[upper], block_hbm.at[upper])
     keep(grad_out_ref.at[upper], grad_hbm.at[upper])
     turns[1].collect(f_ref)
+    turns[2].collect(f_ref)
     share.start()
     inner = jnp.broadcast_to(linear, (4, 48, C)) > 0
     halo_u.wait_recv()
@@ -645,14 +653,15 @@
         pltpu.VMEM((C, C), BF16),
         pltpu.VMEM((768, 128), F32),
         pltpu.VMEM((8, 16, 128), F32),
-        pltpu.VMEM((NZ, 16, 128), F32),
+        pltpu.VMEM((8, 16, 128), BF16),
+        pltpu.VMEM((NZ, 16, 128), BF16),
         dma((15,)), dma((5,)), dma((5,)), dma((5,)), dma((8,)), dma((NZ,)),
         pltpu.SemaphoreType.REGULAR((5,)),
     ]
     for rows in GROUPS:
         scratch += group_scratch(len(rows))
-    for members in TURNS:
-        scratch += turn_scratch()
+    for rows in GROUPS:
+        scratch += turn_scratch(len(rows))
     block_out, token_grad, red = pl.pallas_call(
         kernel,
         out_shape=[grid, grid, jax.ShapeDtypeStruct((16, 128), F32)],

time: 53 us -> 52.4 us (0.989)
  Pallas kernels: 52.2 us -> 51.6 us
    pallas_call x1, Pallas kernels: 49.7 us -> 49.2 us  [local(): pl.pallas_call(kernel, out_shape=[grid, grid, jax.ShapeDtypeStruct((16, 1...]
where the time goes in v7:
time: 52.4 us; the launch traced here: 52.3 us
  Pallas kernels  51.6 us (98%)
  between operations  0.64 us (1%)
    pallas_call x1, Pallas kernels, local(): pl.pallas_call(kernel, out_shape=[grid, grid, jax.ShapeDtypeStruct((16, 1...  49.2 us
    pallas_call x1, Pallas kernels, local(): pl.pallas_call(place_kernel, out_shape=[grid, grid] + [jax.ShapeDtypeStru...  2.46 us

profile of v7, /device:TPU:1, one launch (start us, length us, event | category | flops | bytes accessed | tf_op | source)
XLA Modules:
  0.0 52.3 jit_solution(17285168542619124364)
XLA Ops:
  0.6 49.2 %window_block.1 = (bf16[8,48,384]{2,1,0:T(8,128)(2,1)}, bf16[8,48,384]{2,1,0:T(8,128)(2,1)}, f32[16,128]{1,0:T(8,128)}) custom-call(bf16[8,48,384]{2,1,0:T(8,128)(2,1)} %tok_hbm.1, bf16[8,48,384]{2,1,0:T(8,128)(2,1)} %cot_hbm.1, s32[8,48]{1,0:T(8,128)} %oce_hbm.1, s32[1,6]{1,0:T(1,128)} %land_hbm.1, bf16[384,1152]{1,0:T(8,128)(2,1)} %wqkv_hbm.1, ...), custom_call_target="tpu_custom_call" | custom-call | flops 1500000000 | bytes 5000000 | tf_op jit(solution)/shard_map/window_block/pallas_call | solution.py:665
  49.8 2.5 %outputs.1 = (bf16[8,48,384]{2,1,0:T(8,128)(2,1)}, bf16[8,48,384]{2,1,0:T(8,128)(2,1)}, f32[864]{0:T(1024)}, f32[288]{0:T(512)}, f32[96]{0:T(128)}) custom-call(bf16[8,48,384]{2,1,0:T(8,128)(2,1)} %get-tuple-element.8.block_hbm, bf16[8,48,384]{2,1,0:T(8,128)(2,1)} %get-tuple-element.9.grad_hbm, f32[16,128]{1,0:T(8,128)} %get-tuple-element.10.red_hbm), custom_call_target="tpu_custom_call" | custom-call | flops 10000 | bytes 1200000 | tf_op jit(solution)/shard_map/outputs/pallas_call | solution.py:681

commit v8 on v7

--- a/solution.py
+++ b/solution.py
@@ -30,6 +30,8 @@
 BIAS_ROWS = [("bias", j, 0) for j in range(3)]
 GROUPS = [PROJ_ROWS + qkv_rows(0), qkv_rows(1)[:8], qkv_rows(1)[8:] + qkv_rows(2) + BIAS_ROWS]
 SLOTS = 13
+X_ORDER = (2, 1, 3)
+Y_ORDER = (4, 3, 5, 2, 6, 1, 7)
 
 
 def owned(g):
@@ -82,51 +84,44 @@
 
 
 class Group:
-    def __init__(self, rows, refs, here, send):
-        self.rows, self.n, self.here, self.send = rows, len(rows), here, send
-        (
-            self.pk, self.pack, self.r0, self.s1, self.rx,
-            self.core_s, self.core_r, self.x_s, self.x_r,
-        ) = refs
+    def __init__(self, rows, base, pk_ref, refs, here, plan):
+        self.rows, self.n, self.base, self.pk = rows, len(rows), base, pk_ref
+        self.pack, self.r0, self.s1, self.rx, core_s, core_r, x_s, x_r = refs
+        band, grp, y, x, z, core = here
+        self.theirs = pl.ds(pl.multiple_of((1 - core) * 64, 64), 64)
+        self.mine = pl.ds(pl.multiple_of(core * 64, 64), 64)
+        self.own = pl.ds(pl.multiple_of(16 * x, 16), 16)
+        self.core_copy = plan(self.pack, self.r0, core_s.at[0], core_r.at[0], (band, z * 2 + 1 - core))
+        self.sent = []
+        for d in X_ORDER:
+            to = lax.rem(x + d, NX)
+            part = self.s1.at[:, pl.ds(pl.multiple_of(16 * to, 16), 16), :]
+            self.sent.append(plan(part, self.rx.at[d - 1], x_s.at[d - 1], x_r.at[d - 1], (y * NX + to, grp)))
 
     def start(self):
-        band, grp, y, x, z, core = self.here
-        theirs = pl.ds(pl.multiple_of((1 - core) * 64, 64), 64)
-
         def narrow(i, carry):
-            self.pack[i] = self.pk[i, theirs, :].astype(BF16)
+            self.pack[i] = self.pk[self.base + i, self.theirs, :].astype(BF16)
             return carry
 
-        lax.fori_loop(0, self.n, narrow, 0, unroll=3)
-        self.core_copy = self.send(
-            self.pack, self.r0, self.core_s.at[0], self.core_r.at[0], (band, z * 2 + 1 - core)
-        )
+        lax.fori_loop(0, self.n, narrow, 0, unroll=2)
+        self.core_copy.start()
 
     def spread(self):
-        band, grp, y, x, z, core = self.here
-        mine = pl.ds(pl.multiple_of(core * 64, 64), 64)
         self.core_copy.wait()
 
         def add(i, carry):
-            self.s1[i] = (self.pk[i, mine, :] + self.r0[i].astype(F32)).astype(BF16)
+            total = self.pk[self.base + i, self.mine, :] + self.r0[i].astype(F32)
+            self.s1[i] = total.astype(BF16)
             return carry
 
-        lax.fori_loop(0, self.n, add, 0, unroll=3)
-        self.sent = []
-        for d in range(1, NX):
-            to = lax.rem(x + d, NX)
-            self.sent.append(
-                self.send(
-                    self.s1.at[:, pl.ds(pl.multiple_of(16 * to, 16), 16), :], self.rx.at[d - 1],
-                    self.x_s.at[d - 1], self.x_r.at[d - 1], (y * NX + to, grp),
-                )
-            )
+        lax.fori_loop(0, self.n, add, 0, unroll=2)
+        for copy in self.sent:
+            copy.start()
 
     def take(self, wide_ref, padded):
-        band, grp, y, x, z, core = self.here
-        total = self.s1[:, pl.ds(pl.multiple_of(16 * x, 16), 16), :].astype(F32)
-        for d in range(1, NX):
-            self.sent[d - 1].wait_recv()
+        total = self.s1[:, self.own, :].astype(F32)
+        for copy, d in zip(self.sent, X_ORDER):
+            copy.wait_recv()
             total = total + self.rx[d - 1].astype(F32)
         for i in range(self.n):
             for quarter in range(2):
@@ -139,10 +134,18 @@
 
 
 class Turn:
-    def __init__(self, group, refs, here, send):
-        self.group, self.here, self.send = group, here, send
-        self.rows, self.padded = group.rows, padded_of(group.n)
-        self.wide, self.tb, self.ry, self.y_s, self.y_r = refs
+    def __init__(self, group, refs, here, plan):
+        self.group, self.rows, self.padded = group, group.rows, padded_of(group.n)
+        self.wide, self.tb, self.ry, y_s, y_r = refs
+        band, grp, y, x, z, core = here
+        n = 2 * self.padded
+        self.own = pl.ds(pl.multiple_of(y * n, 8), n)
+        self.sent = []
+        for d in Y_ORDER:
+            to = lax.rem(y + d, NY)
+            self.sent.append(
+                plan(self.tb.at[to], self.ry.at[d - 1], y_s.at[d - 1], y_r.at[d - 1], (to * NX + x, grp))
+            )
 
     def clear(self):
         for i in range(len(self.rows), self.padded):
@@ -151,27 +154,17 @@
                 self.wide[at, :] = jnp.zeros((NY, 128), F32)
 
     def start(self):
-        band, grp, y, x, z, core = self.here
         n = 2 * self.padded
         self.group.take(self.wide, self.padded)
         for i in range(NY):
             self.tb[i] = self.wide[n * i : n * (i + 1), :].astype(BF16)
-        self.sent = []
-        for d in range(1, NY):
-            to = lax.rem(y + d, NY)
-            self.sent.append(
-                self.send(
-                    self.tb.at[to], self.ry.at[d - 1],
-                    self.y_s.at[d - 1], self.y_r.at[d - 1], (to * NX + x, grp),
-                )
-            )
+        for copy in self.sent:
+            copy.start()
 
     def collect(self, f_ref):
-        band, grp, y, x, z, core = self.here
-        n = 2 * self.padded
-        total = self.wide[pl.ds(pl.multiple_of(y * n, 8), n), :]
-        for d in range(1, NY):
-            self.sent[d - 1].wait_recv()
+        total = self.wide[self.own, :]
+        for copy, d in zip(self.sent, Y_ORDER):
+            copy.wait_recv()
             total = total + self.ry[d - 1].astype(F32)
         for i in range(8):
             for at, row in enumerate(owned(i % 4)):
@@ -236,7 +229,6 @@
 def group_scratch(n):
     dma = pltpu.SemaphoreType.DMA
     return [
-        pltpu.VMEM((n, 128, 128), F32),
         pltpu.VMEM((n, 64, 128), BF16),
         pltpu.VMEM((n, 64, 128), BF16),
         pltpu.VMEM((n, 64, 128), BF16),
@@ -274,7 +266,7 @@
     tok_ref, cot_ref, oce_ref, land_ref, wqkv_ref, wproj_ref, rb_ref,
     htok_ref, hcot_ref, hoce_ref, uu_ref, ug_ref, hu_ref, hg_ref,
     x_ref, c_ref, n_ref, inv_ref, mask_ref, h_ref, ht_ref, qkv_ref, dz_ref, do_ref, o_ref, dqkv_ref, ot_ref,
-    p_ref, bias_ref, db_ref, perm_ref, bt_ref, f_ref, low_ref, r3_ref, load_sem, store_sem, halo_s, halo_r, z_s, z_r, near_sem, *rest,
+    p_ref, bias_ref, db_ref, perm_ref, pk_ref, bt_ref, f_ref, low_ref, r3_ref, load_sem, store_sem, halo_s, halo_r, z_s, z_r, near_sem, *rest,
 ):
     band = lax.axis_index("band")
     grp = lax.axis_index("grp")
@@ -319,10 +311,13 @@
         for to in (at(d), at(-d)):
             pl.semaphore_signal(near_sem.at[r], inc=1, device_id=to, device_id_type=MESH)
 
-    def send(src, dst, s, r, to):
-        copy = pltpu.make_async_remote_copy(
+    def plan(src, dst, s, r, to):
+        return pltpu.make_async_remote_copy(
             src_ref=src, dst_ref=dst, send_sem=s, recv_sem=r, device_id=to, device_id_type=MESH
         )
+
+    def send(*args):
+        copy = plan(*args)
         copy.start()
         return copy
 
@@ -360,7 +355,13 @@
 
     def project(half):
         rows = slice(OWN * half, OWN * half + OWN)
-        qkv_ref[rows, :] = dot_nn(h_ref[rows, :], wqkv_ref[...]).astype(BF16)
+
+        def part(g, carry):
+            lanes = pl.ds(pl.multiple_of(C * g, 128), C)
+            qkv_ref[rows, lanes] = dot_nn(h_ref[rows, :], wqkv_ref[:, lanes]).astype(BF16)
+            return carry
+
+        lax.fori_loop(0, HG, part, 0)
 
     def pull(half):
         rows = slice(OWN * half, OWN * half + OWN)
@@ -428,31 +429,32 @@
         ref[second, lanes] = value[32:64]
 
     def lanes_of(g):
-        return [slice(C * g + 128 * i, C * g + 128 * i + 128) for i in range(3)] + [
-            slice(256 * g, 256 * g + 256)
+        return [pl.ds(pl.multiple_of(C * g + 128 * i, 128), 128) for i in range(3)] + [
+            pl.ds(pl.multiple_of(256 * g, 256), 256),
+            pl.ds(pl.multiple_of(128 * g, 128), 128),
         ]
 
     def forward(w, carry):
         whole = pl.ds(pl.multiple_of(w * 64, 64), 64)
         live = jnp.concatenate([load(mask_ref, w, slice(0, 128))] * 2, 1) > 0.5
         for g in range(HG):
-            q_lanes, k_lanes, v_lanes, wide = lanes_of(g)
+            q_lanes, k_lanes, v_lanes, wide, head_lanes = lanes_of(g)
             q4 = spread(load(qkv_ref, w, q_lanes))
             s = dot_nt(load(qkv_ref, w, k_lanes), q4) * SCALE + bias_ref[:, wide]
             s = jnp.where(live, s, MASKED)
             weights = jnp.exp(s - jnp.max(s, 0, keepdims=True))
             p = weights * (1.0 / jnp.sum(weights, 0, keepdims=True))
             p_ref[whole, wide] = p
-            store(o_ref, w, slice(128 * g, 128 * g + 128), fold(dot_tn(p.astype(BF16), load(qkv_ref, w, v_lanes))).astype(BF16))
+            store(o_ref, w, head_lanes, fold(dot_tn(p.astype(BF16), load(qkv_ref, w, v_lanes))).astype(BF16))
         return carry
 
     def backward(g):
-        q_lanes, k_lanes, v_lanes, wide = lanes_of(g)
+        q_lanes, k_lanes, v_lanes, wide, head_lanes = lanes_of(g)
 
         def step(w, carry):
             whole = pl.ds(pl.multiple_of(w * 64, 64), 64)
             q4 = spread(load(qkv_ref, w, q_lanes))
-            do4 = spread(load(do_ref, w, slice(128 * g, 128 * g + 128)))
+            do4 = spread(load(do_ref, w, head_lanes))
             p = p_ref[whole, wide]
             dp = dot_nt(load(qkv_ref, w, v_lanes), do4)
             store(dqkv_ref, w, v_lanes, dot_nn(p.astype(BF16), do4).astype(BF16))
@@ -465,7 +467,7 @@
             return carry
 
         lax.fori_loop(0, WB, step, 0, unroll=6)
-        fill(qkv_rows(g), dot_nn(ht_ref[...], dqkv_ref[:, C * g : C * g + C]))
+        fill(9 + 9 * g, dot_nn(ht_ref[...], dqkv_ref[:, pl.ds(pl.multiple_of(C * g, 128), C)]))
 
     lax.fori_loop(0, WB, forward, 0, unroll=2)
 
@@ -475,37 +477,45 @@
 
     here = (band, grp, y, x, z, core)
     groups, turns = [], []
-    at = 0
+    at = base = 0
     for rows in GROUPS:
-        groups.append(Group(rows, rest[at : at + 9], here, send))
-        at += 9
+        groups.append(Group(rows, base, pk_ref, rest[at : at + 8], here, plan))
+        at += 8
+        base += len(rows)
     for group in groups:
-        turns.append(Turn(group, rest[at : at + 5], here, send))
+        turns.append(Turn(group, rest[at : at + 5], here, plan))
         at += 5
     share = Share(f_ref, low_ref, r3_ref, z_s, z_r, here)
 
-    def fill(rows, value):
-        for i, row in enumerate(rows):
-            j, k = i % 3, i // 3
-            for group in groups:
-                if row in group.rows:
-                    at = group.rows.index(row)
-                    group.pk[at] = value[128 * j : 128 * j + 128, 128 * k : 128 * k + 128]
+    def fill(base, value):
+        for k in range(3):
+            for j in range(3):
+                pk_ref[base + 3 * k + j] = value[128 * j : 128 * j + 128, 128 * k : 128 * k + 128]
 
     ot_ref[...] = dot_nt(perm_ref[...], o_ref[...]).astype(BF16)
-    fill(PROJ_ROWS, dot_nn(ot_ref[...], dz_ref[...]))
-    backward(0)
-    groups[0].start()
+    fill(0, dot_nn(ot_ref[...], dz_ref[...]))
+    for turn in turns:
+        turn.clear()
     for i in range(8):
         f_ref[i, SLOTS:16, :] = jnp.zeros((16 - SLOTS, 128), F32)
-    for turn in turns:
-        turn.clear()
-    backward(1)
-    groups[1].start()
-    for r in far:
-        pl.semaphore_wait(near_sem.at[r], 2)
-    groups[0].spread()
-    backward(2)
+
+    def heads(g, carry):
+        backward(g)
+
+        @pl.when(g == 0)
+        def _():
+            groups[0].start()
+
+        @pl.when(g == 1)
+        def _():
+            groups[1].start()
+            for r in far:
+                pl.semaphore_wait(near_sem.at[r], 2)
+            groups[0].spread()
+
+        return carry
+
+    lax.fori_loop(0, HG, heads, 0)
     for i in range(6):
         bt_ref[128 * i : 128 * i + 128, 0:64] = db_ref[:, 128 * i : 128 * i + 128].T
     lane = lax.broadcasted_iota(jnp.int32, (8, 128), 1)
@@ -514,7 +524,7 @@
             first = 2 * j + 24 * ((i // 2) % 4) + 12 * (i // 8) + 6 * (i % 2)
             even = bt_ref[pl.ds(first, 8, stride=96), :]
             odd = bt_ref[pl.ds(first + 1, 8, stride=96), :]
-            groups[2].pk[groups[2].n - 3 + j, 8 * i : 8 * i + 8, :] = jnp.where(lane < 64, even, pltpu.roll(odd, 64, 1))
+            pk_ref[36 + j, 8 * i : 8 * i + 8, :] = jnp.where(lane < 64, even, pltpu.roll(odd, 64, 1))
     groups[2].start()
     groups[1].spread()
 
@@ -651,6 +661,7 @@
         pltpu.VMEM((64, 768), F32),
         pltpu.VMEM((64, 768), F32),
         pltpu.VMEM((C, C), BF16),
+        pltpu.VMEM((39, 128, 128), F32),
         pltpu.VMEM((768, 128), F32),
         pltpu.VMEM((8, 16, 128), F32),
         pltpu.VMEM((8, 16, 128), BF16),

time: 52.4 us -> 51 us (0.973)
  Pallas kernels: 51.6 us -> 50.2 us
    pallas_call x1, Pallas kernels: 49.2 us -> 47.7 us  [local(): pl.pallas_call(kernel, out_shape=[grid, grid, jax.ShapeDtypeStruct((16, 1...]
where the time goes in v8:
time: 51 us; the launch traced here: 50.8 us
  Pallas kernels  50.2 us (98%)
  between operations  0.64 us (1%)
    pallas_call x1, Pallas kernels, local(): pl.pallas_call(kernel, out_shape=[grid, grid, jax.ShapeDtypeStruct((16, 1...  47.7 us
    pallas_call x1, Pallas kernels, local(): pl.pallas_call(place_kernel, out_shape=[grid, grid] + [jax.ShapeDtypeStru...  2.46 us

profile of v8, /device:TPU:1, one launch (start us, length us, event | category | flops | bytes accessed | tf_op | source)
XLA Modules:
  0.0 50.8 jit_solution(17835884228185782455)
XLA Ops:
  0.6 47.7 %window_block.1 = (bf16[8,48,384]{2,1,0:T(8,128)(2,1)}, bf16[8,48,384]{2,1,0:T(8,128)(2,1)}, f32[16,128]{1,0:T(8,128)}) custom-call(bf16[8,48,384]{2,1,0:T(8,128)(2,1)} %tok_hbm.1, bf16[8,48,384]{2,1,0:T(8,128)(2,1)} %cot_hbm.1, s32[8,48]{1,0:T(8,128)} %oce_hbm.1, s32[1,6]{1,0:T(1,128)} %land_hbm.1, bf16[384,1152]{1,0:T(8,128)(2,1)} %wqkv_hbm.1, ...), custom_call_target="tpu_custom_call" | custom-call | flops 1500000000 | bytes 5000000 | tf_op jit(solution)/shard_map/window_block/pallas_call | solution.py:676
  48.4 2.5 %outputs.1 = (bf16[8,48,384]{2,1,0:T(8,128)(2,1)}, bf16[8,48,384]{2,1,0:T(8,128)(2,1)}, f32[864]{0:T(1024)}, f32[288]{0:T(512)}, f32[96]{0:T(128)}) custom-call(bf16[8,48,384]{2,1,0:T(8,128)(2,1)} %get-tuple-element.8.block_hbm, bf16[8,48,384]{2,1,0:T(8,128)(2,1)} %get-tuple-element.9.grad_hbm, f32[16,128]{1,0:T(8,128)} %get-tuple-element.10.red_hbm), custom_call_target="tpu_custom_call" | custom-call | flops 10000 | bytes 1200000 | tf_op jit(solution)/shard_map/outputs/pallas_call | solution.py:692

commit v9 on v8

--- a/solution.py
+++ b/solution.py
@@ -32,6 +32,7 @@
 SLOTS = 13
 X_ORDER = (2, 1, 3)
 Y_ORDER = (4, 3, 5, 2, 6, 1, 7)
+Z_ORDER = (4, 3, 5, 2, 6, 1, 7, 0)
 
 
 def owned(g):
@@ -177,24 +178,28 @@
     def __init__(self, wide_ref, f_ref, r3_ref, z_s, z_r, here):
         self.wide, self.f, self.r3, self.z_s, self.z_r, self.here = wide_ref, f_ref, r3_ref, z_s, z_r, here
 
-    def last(self, i):
+    def copies(self):
         band, grp, y, x, z, core = self.here
-        quarter, zi, to_core = i // 4, (i // 2) % 2, i % 2
-        to_z = 2 * (2 * core + quarter) + zi
-        copy = pltpu.make_async_remote_copy(
-            src_ref=self.f.at[i],
-            dst_ref=self.r3.at[z],
-            send_sem=self.z_s.at[i],
-            recv_sem=self.z_r.at[z],
-            device_id=(band, to_z * 2 + to_core),
-            device_id_type=MESH,
-        )
-        return copy, jnp.logical_or(to_z != z, core != to_core)
+        for d in Z_ORDER:
+            to_z = lax.rem(z + d, NZ)
+            for to_core in range(2):
+                i = 2 * lax.rem(to_z, 4) + to_core
+                copy = pltpu.make_async_remote_copy(
+                    src_ref=self.f.at[i],
+                    dst_ref=self.r3.at[z],
+                    send_sem=self.z_s.at[i],
+                    recv_sem=self.z_r.at[z],
+                    device_id=(band, to_z * 2 + to_core),
+                    device_id_type=MESH,
+                )
+                away = to_z // 4 == core
+                if d == 0:
+                    away = jnp.logical_and(away, core != to_core)
+                yield copy, away
 
     def start(self):
         self.f[...] = self.wide[...].astype(BF16)
-        for i in range(8):
-            copy, away = self.last(i)
+        for copy, away in self.copies():
             pl.when(away)(copy.start)
 
     def finish(self, red_ref):
@@ -221,8 +226,7 @@
         red_ref[...] = total
 
     def drain(self):
-        for i in range(8):
-            copy, away = self.last(i)
+        for copy, away in self.copies():
             pl.when(away)(copy.wait_send)
 
 
@@ -355,13 +359,7 @@
 
     def project(half):
         rows = slice(OWN * half, OWN * half + OWN)
-
-        def part(g, carry):
-            lanes = pl.ds(pl.multiple_of(C * g, 128), C)
-            qkv_ref[rows, lanes] = dot_nn(h_ref[rows, :], wqkv_ref[:, lanes]).astype(BF16)
-            return carry
-
-        lax.fori_loop(0, HG, part, 0)
+        qkv_ref[rows, :] = dot_nn(h_ref[rows, :], wqkv_ref[...]).astype(BF16)
 
     def pull(half):
         rows = slice(OWN * half, OWN * half + OWN)
@@ -429,9 +427,9 @@
         ref[second, lanes] = value[32:64]
 
     def lanes_of(g):
-        return [pl.ds(pl.multiple_of(C * g + 128 * i, 128), 128) for i in range(3)] + [
-            pl.ds(pl.multiple_of(256 * g, 256), 256),
-            pl.ds(pl.multiple_of(128 * g, 128), 128),
+        return [slice(C * g + 128 * i, C * g + 128 * i + 128) for i in range(3)] + [
+            slice(256 * g, 256 * g + 256),
+            slice(128 * g, 128 * g + 128),
         ]
 
     def forward(w, carry):
@@ -467,7 +465,7 @@
             return carry
 
         lax.fori_loop(0, WB, step, 0, unroll=6)
-        fill(9 + 9 * g, dot_nn(ht_ref[...], dqkv_ref[:, pl.ds(pl.multiple_of(C * g, 128), C)]))
+        fill(9 + 9 * g, dot_nn(ht_ref[...], dqkv_ref[:, C * g : C * g + C]))
 
     lax.fori_loop(0, WB, forward, 0, unroll=2)
 
@@ -499,23 +497,14 @@
     for i in range(8):
         f_ref[i, SLOTS:16, :] = jnp.zeros((16 - SLOTS, 128), F32)
 
-    def heads(g, carry):
-        backward(g)
-
-        @pl.when(g == 0)
-        def _():
-            groups[0].start()
-
-        @pl.when(g == 1)
-        def _():
-            groups[1].start()
-            for r in far:
-                pl.semaphore_wait(near_sem.at[r], 2)
-            groups[0].spread()
-
-        return carry
-
-    lax.fori_loop(0, HG, heads, 0)
+    backward(0)
+    groups[0].start()
+    backward(1)
+    groups[1].start()
+    for r in far:
+        pl.semaphore_wait(near_sem.at[r], 2)
+    groups[0].spread()
+    backward(2)
     for i in range(6):
         bt_ref[128 * i : 128 * i + 128, 0:64] = db_ref[:, 128 * i : 128 * i + 128].T
     lane = lax.broadcasted_iota(jnp.int32, (8, 128), 1)
@@ -587,7 +576,7 @@
 
 def place_kernel(
     block_hbm, grad_hbm, red_hbm, block_out, grad_out, qkv_out, proj_out, bias_out,
-    block_ref, grad_ref, red_ref, in_sem, out_sem,
+    block_ref, grad_ref, red_ref, qkv_ref, proj_ref, bias_ref, in_sem, out_sem,
 ):
     load = pltpu.make_async_copy(red_hbm, red_ref, in_sem.at[4])
     load.start()
@@ -599,9 +588,6 @@
             into.start()
             moves.append((into, pltpu.make_async_copy(via.at[part], dst.at[part], out_sem.at[2 * i + j])))
     load.wait()
-    for into, out in moves:
-        into.wait()
-        out.start()
     g = lax.rem(lax.axis_index("grp"), 4)
     lane = lax.broadcasted_iota(jnp.int32, (16, 128), 1)
     red = red_ref[...]
@@ -619,12 +605,24 @@
             value = jnp.where(which == quarter, rolled[quarter], value)
         return value
 
-    for out, step, first, size in ((qkv_out, 27, 0, 864), (proj_out, 9, 8, 288), (bias_out, 3, 11, 96)):
+    for into, out in moves:
+        into.wait()
+        out.start()
+    small = []
+    for i, (ref, out, step, first, size) in enumerate(
+        (
+            (qkv_ref, qkv_out, 27, 0, 864),
+            (proj_ref, proj_out, 9, 8, 288),
+            (bias_ref, bias_out, 3, 11, 96),
+        )
+    ):
         value = pick(step)
-        for i in range(-(-size // 128)):
-            n = min(128, size - 128 * i)
-            out[pl.ds(128 * i, n)] = value[first + i, 0:n]
-    for into, out in moves:
+        for j in range(-(-size // 128)):
+            n = min(128, size - 128 * j)
+            ref[pl.ds(128 * j, n)] = value[first + j, 0:n]
+        small.append(pltpu.make_async_copy(ref, out, out_sem.at[4 + i]))
+        small[-1].start()
+    for out in [out for into, out in moves] + small:
         out.wait()
 
 
@@ -686,20 +684,22 @@
         name="window_block",
     )(tokens, cotangent, ocean_mask, land_mask, w_qkv, w_proj, rel_bias)
 
-    whole = pl.BlockSpec(memory_space=pltpu.VMEM)
     hbm = pl.BlockSpec(memory_space=pltpu.HBM)
     return tuple(
         pl.pallas_call(
             place_kernel,
             out_shape=[grid, grid] + [jax.ShapeDtypeStruct((n,), F32) for n in (864, 288, 96)],
             in_specs=[hbm] * 3,
-            out_specs=[hbm, hbm, whole, whole, whole],
+            out_specs=[hbm] * 5,
             scratch_shapes=[
                 pltpu.VMEM((8, 48, C), BF16),
                 pltpu.VMEM((8, 48, C), BF16),
                 pltpu.VMEM((16, 128), F32),
+                pltpu.VMEM((864,), F32),
+                pltpu.VMEM((288,), F32),
+                pltpu.VMEM((96,), F32),
                 dma((5,)),
-                dma((4,)),
+                dma((7,)),
             ],
             compiler_params=pltpu.CompilerParams(vmem_limit_bytes=VMEM_BYTES),
             cost_estimate=pl.CostEstimate(flops=10**4, bytes_accessed=12 * 10**5, transcendentals=0),

time: 51 us -> 50.2 us (0.984)
  Pallas kernels: 50.2 us -> 49.4 us
    pallas_call x1, Pallas kernels: 2.46 us -> 1.91 us  [local(): pl.pallas_call(place_kernel, out_shape=[grid, grid] + [jax.ShapeDtypeStru...]
where the time goes in v9:
time: 50.2 us; the launch traced here: 50.1 us
  Pallas kernels  49.4 us (98%)
  between operations  0.64 us (1%)
    pallas_call x1, Pallas kernels, local(): pl.pallas_call(kernel, out_shape=[grid, grid, jax.ShapeDtypeStruct((16, 1...  47.5 us
    pallas_call x1, Pallas kernels, local(): pl.pallas_call(place_kernel, out_shape=[grid, grid] + [jax.ShapeDtypeStru...  1.91 us

profile of v9, /device:TPU:1, one launch (start us, length us, event | category | flops | bytes accessed | tf_op | source)
XLA Modules:
  0.0 50.1 jit_solution(4622198408876149066)
XLA Ops:
  0.6 47.5 %window_block.1 = (bf16[8,48,384]{2,1,0:T(8,128)(2,1)}, bf16[8,48,384]{2,1,0:T(8,128)(2,1)}, f32[16,128]{1,0:T(8,128)}) custom-call(bf16[8,48,384]{2,1,0:T(8,128)(2,1)} %tok_hbm.1, bf16[8,48,384]{2,1,0:T(8,128)(2,1)} %cot_hbm.1, s32[8,48]{1,0:T(8,128)} %oce_hbm.1, s32[1,6]{1,0:T(1,128)} %land_hbm.1, bf16[384,1152]{1,0:T(8,128)(2,1)} %wqkv_hbm.1, ...), custom_call_target="tpu_custom_call" | custom-call | flops 1500000000 | bytes 5000000 | tf_op jit(solution)/shard_map/window_block/pallas_call | solution.py:674
  48.2 1.9 %outputs.1 = (bf16[8,48,384]{2,1,0:T(8,128)(2,1)}, bf16[8,48,384]{2,1,0:T(8,128)(2,1)}, f32[864]{0:T(1024)}, f32[288]{0:T(512)}, f32[96]{0:T(128)}) custom-call(bf16[8,48,384]{2,1,0:T(8,128)(2,1)} %get-tuple-element.8.block_hbm, bf16[8,48,384]{2,1,0:T(8,128)(2,1)} %get-tuple-element.9.grad_hbm, f32[16,128]{1,0:T(8,128)} %get-tuple-element.10.red_hbm), custom_call_target="tpu_custom_call" | custom-call | flops 10000 | bytes 1200000 | tf_op jit(solution)/shard_map/outputs/pallas_call | solution.py:689

commit v10 on v9

--- a/solution.py
+++ b/solution.py
@@ -23,12 +23,13 @@
 
 
 def qkv_rows(g):
-    return [("qkv", j, k) for k in (g, 3 + g, 6 + g) for j in range(3)]
+    return [("qkv", j, k) for k in (g, 3 + g) for j in range(3)]
 
 
 PROJ_ROWS = [("proj", j, k) for k in range(3) for j in range(3)]
 BIAS_ROWS = [("bias", j, 0) for j in range(3)]
-GROUPS = [PROJ_ROWS + qkv_rows(0), qkv_rows(1)[:8], qkv_rows(1)[8:] + qkv_rows(2) + BIAS_ROWS]
+V_ROWS = [("qkv", j, 6 + g) for g in range(3) for j in range(3)]
+GROUPS = [PROJ_ROWS + V_ROWS, qkv_rows(0) + qkv_rows(1), qkv_rows(2) + BIAS_ROWS]
 SLOTS = 13
 X_ORDER = (2, 1, 3)
 Y_ORDER = (4, 3, 5, 2, 6, 1, 7)
@@ -299,14 +300,15 @@
     for peer in peers:
         pl.semaphore_signal(barrier, inc=1, device_id=peer, device_id_type=MESH)
 
-    def blocks(ref, i, j):
-        return ref.at[:, pl.ds(C * i + 128 * j, 128)]
+    def blocks(i, j):
+        to = 256 * j + 128 * i if i < 2 else 768 + 128 * j
+        return wqkv_hbm.at[:, pl.ds(C * i + 128 * j, 128)], wqkv_ref.at[:, pl.ds(to, 128)]
 
     loads = []
     for i, (src, dst) in enumerate(
         [(tok_hbm, tok_ref), (oce_hbm, oce_ref), (land_hbm, land_ref), (cot_hbm, cot_ref)]
         + [(wproj_hbm, wproj_ref), (rb_hbm, rb_ref)]
-        + [(blocks(wqkv_hbm, i, j), blocks(wqkv_ref, j, i)) for j in range(HG) for i in range(3)]
+        + [blocks(i, j) for j in range(HG) for i in range(3)]
     ):
         loads.append(pltpu.make_async_copy(src, dst, load_sem.at[i]))
         loads[-1].start()
@@ -427,7 +429,8 @@
         ref[second, lanes] = value[32:64]
 
     def lanes_of(g):
-        return [slice(C * g + 128 * i, C * g + 128 * i + 128) for i in range(3)] + [
+        firsts = (256 * g, 256 * g + 128, 768 + 128 * g)
+        return [slice(first, first + 128) for first in firsts] + [
             slice(256 * g, 256 * g + 256),
             slice(128 * g, 128 * g + 128),
         ]
@@ -443,6 +446,8 @@
             weights = jnp.exp(s - jnp.max(s, 0, keepdims=True))
             p = weights * (1.0 / jnp.sum(weights, 0, keepdims=True))
             p_ref[whole, wide] = p
+            do4 = spread(load(do_ref, w, head_lanes))
+            store(dqkv_ref, w, v_lanes, dot_nn(p.astype(BF16), do4).astype(BF16))
             store(o_ref, w, head_lanes, fold(dot_tn(p.astype(BF16), load(qkv_ref, w, v_lanes))).astype(BF16))
         return carry
 
@@ -455,7 +460,6 @@
             do4 = spread(load(do_ref, w, head_lanes))
             p = p_ref[whole, wide]
             dp = dot_nt(load(qkv_ref, w, v_lanes), do4)
-            store(dqkv_ref, w, v_lanes, dot_nn(p.astype(BF16), do4).astype(BF16))
             ds = p * (dp - jnp.sum(p * dp, 0, keepdims=True))
             db_ref[:, wide] += ds
             dsc = (ds * SCALE).astype(BF16)
@@ -465,13 +469,13 @@
             return carry
 
         lax.fori_loop(0, WB, step, 0, unroll=6)
-        fill(9 + 9 * g, dot_nn(ht_ref[...], dqkv_ref[:, C * g : C * g + C]))
-
-    lax.fori_loop(0, WB, forward, 0, unroll=2)
+        fill(18 + 6 * g, dot_nn(ht_ref[...], dqkv_ref[:, 256 * g : 256 * g + 256]))
 
     halos[2].wait_recv()
     stage_rows([jnp.where(here_lower, hcot_ref[i].astype(F32), 0.0) for i in range(4)], 1, c_ref)
     pull(1)
+    lax.fori_loop(0, WB, forward, 0, unroll=2)
+
 
     here = (band, grp, y, x, z, core)
     groups, turns = [], []
@@ -486,7 +490,7 @@
     share = Share(f_ref, low_ref, r3_ref, z_s, z_r, here)
 
     def fill(base, value):
-        for k in range(3):
+        for k in range(value.shape[1] // 128):
             for j in range(3):
                 pk_ref[base + 3 * k + j] = value[128 * j : 128 * j + 128, 128 * k : 128 * k + 128]
 
@@ -497,13 +501,14 @@
     for i in range(8):
         f_ref[i, SLOTS:16, :] = jnp.zeros((16 - SLOTS, 128), F32)
 
+    fill(9, dot_nn(ht_ref[...], dqkv_ref[:, 768 : 768 + C]))
+    groups[0].start()
     backward(0)
-    groups[0].start()
-    backward(1)
-    groups[1].start()
     for r in far:
         pl.semaphore_wait(near_sem.at[r], 2)
     groups[0].spread()
+    backward(1)
+    groups[1].start()
     backward(2)
     for i in range(6):
         bt_ref[128 * i : 128 * i + 128, 0:64] = db_ref[:, 128 * i : 128 * i + 128].T

time: 50.2 us -> 53.5 us (1.066)
  Pallas kernels: 49.4 us -> 52.6 us
    pallas_call x1, Pallas kernels: 47.5 us -> 50.7 us  [local(): pl.pallas_call(kernel, out_shape=[grid, grid, jax.ShapeDtypeStruct((16, 1...]
where the time goes in v10:
time: 53.5 us; the launch traced here: 53.3 us
  Pallas kernels  52.6 us (98%)
  between operations  0.64 us (1%)
    pallas_call x1, Pallas kernels, local(): pl.pallas_call(kernel, out_shape=[grid, grid, jax.ShapeDtypeStruct((16, 1...  50.7 us
    pallas_call x1, Pallas kernels, local(): pl.pallas_call(place_kernel, out_shape=[grid, grid] + [jax.ShapeDtypeStru...  1.91 us

profile of v10, /device:TPU:1, one launch (start us, length us, event | category | flops | bytes accessed | tf_op | source)
XLA Modules:
  0.0 53.3 jit_solution(16746664661026918646)
XLA Ops:
  0.6 50.7 %window_block.1 = (bf16[8,48,384]{2,1,0:T(8,128)(2,1)}, bf16[8,48,384]{2,1,0:T(8,128)(2,1)}, f32[16,128]{1,0:T(8,128)}) custom-call(bf16[8,48,384]{2,1,0:T(8,128)(2,1)} %tok_hbm.1, bf16[8,48,384]{2,1,0:T(8,128)(2,1)} %cot_hbm.1, s32[8,48]{1,0:T(8,128)} %oce_hbm.1, s32[1,6]{1,0:T(1,128)} %land_hbm.1, bf16[384,1152]{1,0:T(8,128)(2,1)} %wqkv_hbm.1, ...), custom_call_target="tpu_custom_call" | custom-call | flops 1500000000 | bytes 5000000 | tf_op jit(solution)/shard_map/window_block/pallas_call | solution.py:679
  51.4 1.9 %outputs.1 = (bf16[8,48,384]{2,1,0:T(8,128)(2,1)}, bf16[8,48,384]{2,1,0:T(8,128)(2,1)}, f32[864]{0:T(1024)}, f32[288]{0:T(512)}, f32[96]{0:T(128)}) custom-call(bf16[8,48,384]{2,1,0:T(8,128)(2,1)} %get-tuple-element.8.block_hbm, bf16[8,48,384]{2,1,0:T(8,128)(2,1)} %get-tuple-element.9.grad_hbm, f32[16,128]{1,0:T(8,128)} %get-tuple-element.10.red_hbm), custom_call_target="tpu_custom_call" | custom-call | flops 10000 | bytes 1200000 | tf_op jit(solution)/shard_map/outputs/pallas_call | solution.py:694

commit v11 on v9

--- a/solution.py
+++ b/solution.py
@@ -467,7 +467,7 @@
         lax.fori_loop(0, WB, step, 0, unroll=6)
         fill(9 + 9 * g, dot_nn(ht_ref[...], dqkv_ref[:, C * g : C * g + C]))
 
-    lax.fori_loop(0, WB, forward, 0, unroll=2)
+    lax.fori_loop(0, WB, forward, 0, unroll=3)
 
     halos[2].wait_recv()
     stage_rows([jnp.where(here_lower, hcot_ref[i].astype(F32), 0.0) for i in range(4)], 1, c_ref)
@@ -517,10 +517,10 @@
     groups[2].start()
     groups[1].spread()
 
+    groups[2].spread()
+    turns[0].start()
     wide_mask = jnp.concatenate([mask_ref[...]] * 3, 1)
     x_ref[...] = wide_mask * dot_nn(o_ref[...], wproj_ref[...])
-    groups[2].spread()
-    turns[0].start()
     for i in range(4):
         uu_ref[i] = grid_row(x_ref, 1, i).astype(BF16)
     c_ref[...] = dot_nt(dqkv_ref[...], wqkv_ref[...])

time: 50.2 us -> 49.7 us (0.990)
  Pallas kernels: 49.4 us -> 48.8 us
    pallas_call x1, Pallas kernels: 47.5 us -> 46.9 us  [local(): pl.pallas_call(kernel, out_shape=[grid, grid, jax.ShapeDtypeStruct((16, 1...]
where the time goes in v11:
time: 49.7 us; the launch traced here: 49.5 us
  Pallas kernels  48.8 us (98%)
  between operations  0.64 us (1%)
    pallas_call x1, Pallas kernels, local(): pl.pallas_call(kernel, out_shape=[grid, grid, jax.ShapeDtypeStruct((16, 1...  46.9 us
    pallas_call x1, Pallas kernels, local(): pl.pallas_call(place_kernel, out_shape=[grid, grid] + [jax.ShapeDtypeStru...  1.91 us

profile of v11, /device:TPU:1, one launch (start us, length us, event | category | flops | bytes accessed | tf_op | source)
XLA Modules:
  0.0 49.5 jit_solution(1990923343883374320)
XLA Ops:
  0.6 46.9 %window_block.1 = (bf16[8,48,384]{2,1,0:T(8,128)(2,1)}, bf16[8,48,384]{2,1,0:T(8,128)(2,1)}, f32[16,128]{1,0:T(8,128)}) custom-call(bf16[8,48,384]{2,1,0:T(8,128)(2,1)} %tok_hbm.1, bf16[8,48,384]{2,1,0:T(8,128)(2,1)} %cot_hbm.1, s32[8,48]{1,0:T(8,128)} %oce_hbm.1, s32[1,6]{1,0:T(1,128)} %land_hbm.1, bf16[384,1152]{1,0:T(8,128)(2,1)} %wqkv_hbm.1, ...), custom_call_target="tpu_custom_call" | custom-call | flops 1500000000 | bytes 5000000 | tf_op jit(solution)/shard_map/window_block/pallas_call | solution.py:674
  47.6 1.9 %outputs.1 = (bf16[8,48,384]{2,1,0:T(8,128)(2,1)}, bf16[8,48,384]{2,1,0:T(8,128)(2,1)}, f32[864]{0:T(1024)}, f32[288]{0:T(512)}, f32[96]{0:T(128)}) custom-call(bf16[8,48,384]{2,1,0:T(8,128)(2,1)} %get-tuple-element.8.block_hbm, bf16[8,48,384]{2,1,0:T(8,128)(2,1)} %get-tuple-element.9.grad_hbm, f32[16,128]{1,0:T(8,128)} %get-tuple-element.10.red_hbm), custom_call_target="tpu_custom_call" | custom-call | flops 10000 | bytes 1200000 | tf_op jit(solution)/shard_map/outputs/pallas_call | solution.py:689

commit v12 on v11

--- a/solution.py
+++ b/solution.py
@@ -467,7 +467,7 @@
         lax.fori_loop(0, WB, step, 0, unroll=6)
         fill(9 + 9 * g, dot_nn(ht_ref[...], dqkv_ref[:, C * g : C * g + C]))
 
-    lax.fori_loop(0, WB, forward, 0, unroll=3)
+    lax.fori_loop(0, WB, forward, 0, unroll=6)
 
     halos[2].wait_recv()
     stage_rows([jnp.where(here_lower, hcot_ref[i].astype(F32), 0.0) for i in range(4)], 1, c_ref)

time: 49.7 us -> 49.1 us (0.988)
  Pallas kernels: 48.8 us -> 48.3 us
    pallas_call x1, Pallas kernels: 46.9 us -> 46.4 us  [local(): pl.pallas_call(kernel, out_shape=[grid, grid, jax.ShapeDtypeStruct((16, 1...]
where the time goes in v12:
time: 49.1 us; the launch traced here: 49 us
  Pallas kernels  48.3 us (98%)
  between operations  0.64 us (1%)
    pallas_call x1, Pallas kernels, local(): pl.pallas_call(kernel, out_shape=[grid, grid, jax.ShapeDtypeStruct((16, 1...  46.4 us
    pallas_call x1, Pallas kernels, local(): pl.pallas_call(place_kernel, out_shape=[grid, grid] + [jax.ShapeDtypeStru...  1.91 us

profile of v12, /device:TPU:1, one launch (start us, length us, event | category | flops | bytes accessed | tf_op | source)
XLA Modules:
  0.0 49.0 jit_solution(15511727110697558723)
XLA Ops:
  0.6 46.4 %window_block.1 = (bf16[8,48,384]{2,1,0:T(8,128)(2,1)}, bf16[8,48,384]{2,1,0:T(8,128)(2,1)}, f32[16,128]{1,0:T(8,128)}) custom-call(bf16[8,48,384]{2,1,0:T(8,128)(2,1)} %tok_hbm.1, bf16[8,48,384]{2,1,0:T(8,128)(2,1)} %cot_hbm.1, s32[8,48]{1,0:T(8,128)} %oce_hbm.1, s32[1,6]{1,0:T(1,128)} %land_hbm.1, bf16[384,1152]{1,0:T(8,128)(2,1)} %wqkv_hbm.1, ...), custom_call_target="tpu_custom_call" | custom-call | flops 1500000000 | bytes 5000000 | tf_op jit(solution)/shard_map/window_block/pallas_call | solution.py:674
  47.1 1.9 %outputs.1 = (bf16[8,48,384]{2,1,0:T(8,128)(2,1)}, bf16[8,48,384]{2,1,0:T(8,128)(2,1)}, f32[864]{0:T(1024)}, f32[288]{0:T(512)}, f32[96]{0:T(128)}) custom-call(bf16[8,48,384]{2,1,0:T(8,128)(2,1)} %get-tuple-element.8.block_hbm, bf16[8,48,384]{2,1,0:T(8,128)(2,1)} %get-tuple-element.9.grad_hbm, f32[16,128]{1,0:T(8,128)} %get-tuple-element.10.red_hbm), custom_call_target="tpu_custom_call" | custom-call | flops 10000 | bytes 1200000 | tf_op jit(solution)/shard_map/outputs/pallas_call | solution.py:689
